TPU v7x, 32 devices: a whole 2x2x4 slice. The times are simulated.
32 devices in a mesh: dp: 4 (over x, core), row: 4 (over z), col: 2 (over y).
Axes of the slice: x: 2, y: 2, z: 4, core: 2. Of those that a mesh axis runs over, the one named last changes fastest.
Arguments:
- tokens: bfloat16 [16, 16, 32, 1152], P('dp', 'row', 'col'), may hold values from -6 to 6
- conditioning: bfloat16 [16, 1152], P('dp'), may hold values from -6 to 6
- heights: int32 [16], P('dp'), may hold values from 8 to 16, as said below
- widths: int32 [16], P('dp'), may hold values from 16 to 32, as said below
- cotangent: bfloat16 [16, 16, 32, 1152], P('dp', 'row', 'col'), may hold values from -6 to 6
- w_mod: bfloat16 [1152, 6912], P(None, ('dp', 'row', 'col')), may hold values from -0.1875 to 0.1875
- b_mod: bfloat16 [6912], P(('dp', 'row', 'col')), may hold values from -2 to 2
- w_qkv: bfloat16 [1152, 3456], P(('dp', 'row', 'col')), may hold values from -0.1875 to 0.1875
- b_qkv: bfloat16 [3456], P(('dp', 'row', 'col')), may hold values from -2 to 2
- query_gain: float32 [72], replicated, may hold values from 0.5 to 1.5
- key_gain: float32 [72], replicated, may hold values from 0.5 to 1.5
- w_proj: bfloat16 [1152, 1152], P(('dp', 'row', 'col')), may hold values from -3 to 3
- b_proj: bfloat16 [1152], P(('dp', 'row', 'col')), may hold values from -2 to 2
- w_gu: bfloat16 [1152, 6144], P(('dp', 'row', 'col')), may hold values from -0.1875 to 0.1875
- b_gu: bfloat16 [6144], P(('dp', 'row', 'col')), may hold values from -2 to 2
- w_down: bfloat16 [3072, 1152], P(('dp', 'row', 'col')), may hold values from -0.109375 to 0.109375
- b_down: bfloat16 [1152], P(('dp', 'row', 'col')), may hold values from -2 to 2
Outputs:
- block_out: bfloat16 [16, 16, 32, 1152], P('dp', 'row', 'col')
- d_tokens: float32 [16, 16, 32, 1152], P('dp', 'row', 'col')
- d_conditioning: float32 [16, 1152], P('dp', ('row', 'col'))
- d_w_mod: float32 [1152, 6912], P(None, ('dp', 'row', 'col'))
- d_b_mod: float32 [6912], P(('dp', 'row', 'col'))
- d_w_qkv: float32 [1152, 3456], P(('dp', 'row', 'col'))
- d_b_query_key: float32 [2304], P(('dp', 'row', 'col'))
- d_b_value: float32 [1152], P(('dp', 'row', 'col'))
- d_query_gain: float32 [72], replicated
- d_key_gain: float32 [72], replicated
- d_w_proj: float32 [1152, 1152], P(('dp', 'row', 'col'))
- d_b_proj: float32 [1152], P(('dp', 'row', 'col'))
- d_w_gu: float32 [1152, 6144], P(('dp', 'row', 'col'))
- d_b_gu: float32 [6144], P(('dp', 'row', 'col'))
- d_w_down: float32 [3072, 1152], P(('dp', 'row', 'col'))
- d_b_down: float32 [1152], P(('dp', 'row', 'col'))
Inputs may be any that keep to these rules, and one draw needn't show every extreme that they name: `heights`: each item's grid height; in every draw some item has exactly 16. `widths`: each item's grid width; in every draw some item has exactly 32.
All inputs are finite; a program needn't handle non-finite values.
Results may differ from a plain program's by a relative error of at most 0.014.
Values may be sent and summed in bfloat16 or wider, within the bound.
A program may use at most 320 MiB of HBM per device.

v0:
```python
import math

import jax
import jax.numpy as jnp
from jax import lax
from jax.sharding import PartitionSpec as P

HEADS = 16
HEAD = 72
FF = 3072


EPSILON = 1e-06
MASKED = -1000000000.0
PRECISE = lax.Precision.HIGHEST


def rope_tables(row_pos, col_pos, head_size):
    half_size = head_size // 2
    lane_index = jnp.arange(head_size)
    pair_index = (lane_index % half_size // 2).astype(jnp.float32)
    frequency = jnp.exp(-math.log(10000.0) * 2.0 * pair_index / half_size)
    places = jnp.where(lane_index[None, :] >= half_size, col_pos[:, None], row_pos[:, None]).astype(
        jnp.float32
    )
    angles = places * frequency[None, :]
    return (jnp.cos(angles), jnp.sin(angles))


def rotate(values):
    pair_view = values.reshape(values.shape[:-1] + (values.shape[-1] // 2, 2))
    turned = jnp.stack((-pair_view[..., 1], pair_view[..., 0]), axis=-1)
    return turned.reshape(values.shape)


def norm_parts(values):
    centered = values - jnp.mean(values, -1, keepdims=True)
    recip = lax.rsqrt(jnp.mean(centered * centered, -1, keepdims=True) + EPSILON)
    return (centered * recip, recip)


def norm_back(gradient, normed, recip):
    return recip * (
        gradient
        - jnp.mean(gradient, -1, keepdims=True)
        - normed * jnp.mean(gradient * normed, -1, keepdims=True)
    )


def head_back(gradient, raw_value, recip, gain_vec):
    scaled = gradient * gain_vec
    gain_grad = jnp.sum(gradient * raw_value * recip, axis=(0, 1, 2))
    raw_grad = recip * scaled - raw_value * (recip * recip * recip) * jnp.mean(
        scaled * raw_value, -1, keepdims=True
    )
    return (raw_grad, gain_grad)


def local(
    tokens,
    conditioning,
    heights,
    widths,
    cotangent,
    w_mod,
    b_mod,
    w_qkv,
    b_qkv,
    query_gain,
    key_gain,
    w_proj,
    b_proj,
    w_gu,
    b_gu,
    w_down,
    b_down,
):
    item_count, tile_rows, tile_cols, model_width = tokens.shape
    tile_span = tile_rows * tile_cols
    n_row = lax.axis_size("row")
    n_col = lax.axis_size("col")
    groups = n_row * n_col
    key_count = tile_span * groups
    inv_root = 1.0 / math.sqrt(HEAD)
    row_at = lax.axis_index("row")
    col_at = lax.axis_index("col")
    local_index = jnp.arange(tile_span)
    query_rows = row_at * tile_rows + local_index // tile_cols
    query_cols = col_at * tile_cols + local_index % tile_cols
    valid_query = (query_rows[None, :] < heights[:, None]) & (query_cols[None, :] < widths[:, None])
    key_index = jnp.arange(key_count)
    key_owner = key_index // tile_span
    key_spot = key_index % tile_span
    key_rows = key_owner // n_col * tile_rows + key_spot // tile_cols
    key_cols = key_owner % n_col * tile_cols + key_spot % tile_cols
    valid_key = (key_rows[None, :] < heights[:, None]) & (key_cols[None, :] < widths[:, None])
    cos_tab, sin_tab = rope_tables(query_rows, query_cols, HEAD)
    cos_four = cos_tab[None, :, None, :]
    sin_four = sin_tab[None, :, None, :]
    cond_f = conditioning.astype(jnp.float32)
    cond_sig = jax.nn.sigmoid(cond_f)
    act_low = (cond_f * cond_sig).astype(jnp.bfloat16)
    gathered = (
        lax.all_gather(w_mod, ("dp", "row", "col"), axis=1, tiled=True),
        lax.all_gather(b_mod, ("dp", "row", "col"), axis=0, tiled=True),
        lax.all_gather(w_qkv, ("dp", "row", "col"), axis=0, tiled=True),
        lax.all_gather(b_qkv, ("dp", "row", "col"), axis=0, tiled=True),
        lax.all_gather(w_proj, ("dp", "row", "col"), axis=0, tiled=True),
        lax.all_gather(b_proj, ("dp", "row", "col"), axis=0, tiled=True),
        lax.all_gather(w_gu, ("dp", "row", "col"), axis=0, tiled=True),
        lax.all_gather(b_gu, ("dp", "row", "col"), axis=0, tiled=True),
        lax.all_gather(w_down, ("dp", "row", "col"), axis=0, tiled=True),
        lax.all_gather(b_down, ("dp", "row", "col"), axis=0, tiled=True),
    )
    (
        w_mod_all,
        b_mod_all,
        w_qkv_all,
        b_qkv_all,
        w_proj_all,
        b_proj_all,
        w_gu_all,
        b_gu_all,
        w_down_all,
        b_down_all,
    ) = gathered
    modul = jnp.dot(act_low, w_mod_all, preferred_element_type=jnp.float32) + b_mod_all.astype(
        jnp.float32
    )
    shift_a, scale_a, gate_a, shift_m, scale_m, gate_m = [
        modul[:, piece * model_width : (piece + 1) * model_width][:, None, :] for piece in range(6)
    ]
    resid_in = tokens.reshape(item_count, tile_span, model_width).astype(jnp.float32)
    normed_a, recip_a = norm_parts(resid_in)
    h_attn = (normed_a * (1.0 + scale_a) + shift_a).astype(jnp.bfloat16)
    qkv_all = jnp.dot(h_attn, w_qkv_all, preferred_element_type=jnp.float32) + b_qkv_all.astype(
        jnp.float32
    )
    query_raw = qkv_all[..., :model_width].reshape(item_count, tile_span, HEADS, HEAD)
    key_raw = qkv_all[..., model_width : 2 * model_width].reshape(
        item_count, tile_span, HEADS, HEAD
    )
    value_raw = qkv_all[..., 2 * model_width :]
    query_recip = lax.rsqrt(jnp.mean(query_raw * query_raw, -1, keepdims=True) + EPSILON)
    key_recip = lax.rsqrt(jnp.mean(key_raw * key_raw, -1, keepdims=True) + EPSILON)
    query_normed = query_raw * query_recip * query_gain
    key_normed = key_raw * key_recip * key_gain
    query_rot = (query_normed * cos_four + rotate(query_normed) * sin_four).astype(jnp.bfloat16)
    key_rot = (key_normed * cos_four + rotate(key_normed) * sin_four).astype(jnp.bfloat16)
    value_low = value_raw.astype(jnp.bfloat16)
    kv_local = jnp.concatenate([key_rot.reshape(item_count, tile_span, model_width), value_low], -1)
    kv_every = lax.all_gather(kv_local, ("row", "col"), axis=1, tiled=True)
    query_heads = query_rot.transpose(2, 0, 1, 3)
    key_part = (
        kv_every[..., :model_width]
        .reshape(item_count, key_count, HEADS, HEAD)
        .transpose(2, 0, 1, 3)
    )
    value_part = (
        kv_every[..., model_width:]
        .reshape(item_count, key_count, HEADS, HEAD)
        .transpose(2, 0, 1, 3)
    )
    key_mask = valid_key[:, None, :]

    def attend(head_block):
        query_h, key_h, value_h = head_block
        scores = (
            jnp.einsum("itd,ikd->itk", query_h, key_h, preferred_element_type=jnp.float32)
            * inv_root
        )
        scores = jnp.where(key_mask, scores, MASKED)
        row_max = jnp.max(scores, -1, keepdims=True)
        exponent = jnp.exp(scores - row_max)
        row_sum = jnp.sum(exponent, -1, keepdims=True)
        probs = (exponent / row_sum).astype(jnp.bfloat16)
        result = jnp.einsum("itk,ikd->itd", probs, value_h, preferred_element_type=jnp.float32)
        return (result, row_max, row_sum)

    attended_heads, max_kept, sum_kept = lax.map(attend, (query_heads, key_part, value_part))
    attended = (
        attended_heads.transpose(1, 2, 0, 3)
        .reshape(item_count, tile_span, model_width)
        .astype(jnp.bfloat16)
    )
    attn_out = jnp.dot(
        attended, w_proj_all, preferred_element_type=jnp.float32
    ) + b_proj_all.astype(jnp.float32)
    resid_mid = resid_in + gate_a * attn_out
    normed_m, recip_m = norm_parts(resid_mid)
    h_mlp = (normed_m * (1.0 + scale_m) + shift_m).astype(jnp.bfloat16)
    gate_up = jnp.dot(h_mlp, w_gu_all, preferred_element_type=jnp.float32) + b_gu_all.astype(
        jnp.float32
    )
    gate_part = gate_up[..., :FF]
    up_part = gate_up[..., FF:]
    gate_sig = jax.nn.sigmoid(gate_part)
    gate_act = gate_part * gate_sig
    hidden = (gate_act * up_part).astype(jnp.bfloat16)
    mlp_out = jnp.dot(hidden, w_down_all, preferred_element_type=jnp.float32) + b_down_all.astype(
        jnp.float32
    )
    mask_f = valid_query[..., None].astype(jnp.float32)
    block_out = ((resid_mid + gate_m * mlp_out) * mask_f).astype(jnp.bfloat16)
    out_grad = cotangent.reshape(item_count, tile_span, model_width).astype(jnp.float32) * mask_f
    d_mlp = (gate_m * out_grad).astype(jnp.bfloat16)
    d_gate_m = jnp.sum(out_grad * mlp_out, 1)
    dw_down = jnp.einsum("itf,itd->fd", hidden, d_mlp, preferred_element_type=jnp.float32)
    db_down = jnp.sum(d_mlp.astype(jnp.float32), (0, 1))
    d_hidden = jnp.einsum("itd,fd->itf", d_mlp, w_down_all, preferred_element_type=jnp.float32)
    d_gate = d_hidden * up_part * gate_sig * (1.0 + gate_part * (1.0 - gate_sig))
    d_up = d_hidden * gate_act
    d_gate_up = jnp.concatenate([d_gate, d_up], -1).astype(jnp.bfloat16)
    dw_gu = jnp.einsum("itd,ite->de", h_mlp, d_gate_up, preferred_element_type=jnp.float32)
    db_gu = jnp.sum(d_gate_up.astype(jnp.float32), (0, 1))
    d_hmlp = jnp.einsum("ite,de->itd", d_gate_up, w_gu_all, preferred_element_type=jnp.float32)
    d_shift_m = jnp.sum(d_hmlp, 1)
    d_scale_m = jnp.sum(d_hmlp * normed_m, 1)
    d_mid = out_grad + norm_back(d_hmlp * (1.0 + scale_m), normed_m, recip_m)
    d_attn = (gate_a * d_mid).astype(jnp.bfloat16)
    d_gate_a = jnp.sum(d_mid * attn_out, 1)
    dw_proj = jnp.einsum("itd,ite->de", attended, d_attn, preferred_element_type=jnp.float32)
    db_proj = jnp.sum(d_attn.astype(jnp.float32), (0, 1))
    d_attended = jnp.einsum(
        "ite,de->itd", d_attn, w_proj_all, preferred_element_type=jnp.float32
    ).astype(jnp.bfloat16)
    d_att_heads = d_attended.reshape(item_count, tile_span, HEADS, HEAD).transpose(2, 0, 1, 3)
    key_back, value_back = (key_part, value_part)

    def attend_back(head_block):
        query_h, key_h, value_h, grad_h, max_h, sum_h = head_block
        scores = (
            jnp.einsum("itd,ikd->itk", query_h, key_h, preferred_element_type=jnp.float32)
            * inv_root
        )
        scores = jnp.where(key_mask, scores, MASKED)
        probs = jnp.exp(scores - max_h) / sum_h
        d_probs = jnp.einsum("itd,ikd->itk", grad_h, value_h, preferred_element_type=jnp.float32)
        delta = jnp.sum(probs * d_probs, -1, keepdims=True)
        d_scores = (probs * (d_probs - delta)).astype(jnp.bfloat16)
        d_query = (
            jnp.einsum("itk,ikd->itd", d_scores, key_h, preferred_element_type=jnp.float32)
            * inv_root
        )
        d_key = (
            jnp.einsum("itk,itd->ikd", d_scores, query_h, preferred_element_type=jnp.float32)
            * inv_root
        )
        d_value = jnp.einsum(
            "itk,itd->ikd", probs.astype(jnp.bfloat16), grad_h, preferred_element_type=jnp.float32
        )
        return (d_query, d_key, d_value)

    dq_heads, dk_heads, dv_heads = lax.map(
        attend_back, (query_heads, key_back, value_back, d_att_heads, max_kept, sum_kept)
    )
    dkv_term = jnp.concatenate(
        [
            dk_heads.transpose(1, 2, 0, 3).reshape(item_count, key_count, model_width),
            dv_heads.transpose(1, 2, 0, 3).reshape(item_count, key_count, model_width),
        ],
        -1,
    )
    dkv_own = lax.psum_scatter(dkv_term, ("row", "col"), scatter_dimension=1, tiled=True)
    d_key_rot = dkv_own[..., :model_width].reshape(item_count, tile_span, HEADS, HEAD)
    d_value = dkv_own[..., model_width:]
    d_query_rot = dq_heads.transpose(1, 2, 0, 3)
    d_query_n = d_query_rot * cos_four - rotate(d_query_rot * sin_four)
    d_key_n = d_key_rot * cos_four - rotate(d_key_rot * sin_four)
    d_query_raw, dq_gain = head_back(d_query_n, query_raw, query_recip, query_gain)
    d_key_raw, dk_gain = head_back(d_key_n, key_raw, key_recip, key_gain)
    gain_total = lax.psum((dq_gain, dk_gain), ("dp", "row", "col"))
    d_qkv = jnp.concatenate(
        [
            d_query_raw.reshape(item_count, tile_span, model_width),
            d_key_raw.reshape(item_count, tile_span, model_width),
            d_value,
        ],
        -1,
    ).astype(jnp.bfloat16)
    dw_qkv = jnp.einsum("itd,ite->de", h_attn, d_qkv, preferred_element_type=jnp.float32)
    db_qkv = jnp.sum(d_qkv.astype(jnp.float32), (0, 1))
    db_query_key = db_qkv[: 2 * model_width]
    db_value = db_qkv[2 * model_width :]
    d_hattn = jnp.einsum("ite,de->itd", d_qkv, w_qkv_all, preferred_element_type=jnp.float32)
    d_shift_a = jnp.sum(d_hattn, 1)
    d_scale_a = jnp.sum(d_hattn * normed_a, 1)
    d_tokens = d_mid + norm_back(d_hattn * (1.0 + scale_a), normed_a, recip_a)
    d_modul = jnp.concatenate([d_shift_a, d_scale_a, d_gate_a, d_shift_m, d_scale_m, d_gate_m], -1)
    act_f = act_low.astype(jnp.float32)
    dw_mod = jnp.einsum("id,ie->de", act_f, d_modul, precision=PRECISE)
    db_mod = jnp.sum(d_modul, 0)
    d_act = jnp.einsum("ie,de->id", d_modul, w_mod_all.astype(jnp.float32), precision=PRECISE)
    d_cond_part = d_act * cond_sig * (1.0 + cond_f * (1.0 - cond_sig))
    d_cond = lax.psum_scatter(d_cond_part, ("row", "col"), scatter_dimension=1, tiled=True)
    summed = (
        lax.psum_scatter(dw_mod, ("dp", "row", "col"), scatter_dimension=1, tiled=True),
        lax.psum_scatter(db_mod, ("dp", "row", "col"), scatter_dimension=0, tiled=True),
        lax.psum_scatter(dw_qkv, ("dp", "row", "col"), scatter_dimension=0, tiled=True),
        lax.psum_scatter(db_query_key, ("dp", "row", "col"), scatter_dimension=0, tiled=True),
        lax.psum_scatter(db_value, ("dp", "row", "col"), scatter_dimension=0, tiled=True),
        lax.psum_scatter(dw_proj, ("dp", "row", "col"), scatter_dimension=0, tiled=True),
        lax.psum_scatter(db_proj, ("dp", "row", "col"), scatter_dimension=0, tiled=True),
        lax.psum_scatter(dw_gu, ("dp", "row", "col"), scatter_dimension=0, tiled=True),
        lax.psum_scatter(db_gu, ("dp", "row", "col"), scatter_dimension=0, tiled=True),
        lax.psum_scatter(dw_down, ("dp", "row", "col"), scatter_dimension=0, tiled=True),
        lax.psum_scatter(db_down, ("dp", "row", "col"), scatter_dimension=0, tiled=True),
    )
    (
        g_w_mod,
        g_b_mod,
        g_w_qkv,
        g_b_query_key,
        g_b_value,
        g_w_proj,
        g_b_proj,
        g_w_gu,
        g_b_gu,
        g_w_down,
        g_b_down,
    ) = summed
    return (
        block_out.reshape(item_count, tile_rows, tile_cols, model_width),
        d_tokens.reshape(item_count, tile_rows, tile_cols, model_width),
        d_cond,
        g_w_mod,
        g_b_mod,
        g_w_qkv,
        g_b_query_key,
        g_b_value,
        gain_total[0],
        gain_total[1],
        g_w_proj,
        g_b_proj,
        g_w_gu,
        g_b_gu,
        g_w_down,
        g_b_down,
    )


def solution(mesh):
    in_specs = (
        P("dp", "row", "col", None),
        P("dp", None),
        P("dp"),
        P("dp"),
        P("dp", "row", "col", None),
        P(None, ("dp", "row", "col")),
        P(("dp", "row", "col")),
        P(("dp", "row", "col"), None),
        P(("dp", "row", "col")),
        P(),
        P(),
        P(("dp", "row", "col"), None),
        P(("dp", "row", "col")),
        P(("dp", "row", "col"), None),
        P(("dp", "row", "col")),
        P(("dp", "row", "col"), None),
        P(("dp", "row", "col")),
    )
    out_specs = (
        P("dp", "row", "col", None),
        P("dp", "row", "col", None),
        P("dp", ("row", "col")),
        P(None, ("dp", "row", "col")),
        P(("dp", "row", "col")),
        P(("dp", "row", "col"), None),
        P(("dp", "row", "col")),
        P(("dp", "row", "col")),
        P(),
        P(),
        P(("dp", "row", "col"), None),
        P(("dp", "row", "col")),
        P(("dp", "row", "col"), None),
        P(("dp", "row", "col")),
        P(("dp", "row", "col"), None),
        P(("dp", "row", "col")),
    )
    return jax.shard_map(local, mesh=mesh, in_specs=in_specs, out_specs=out_specs, check_vma=False)
```

profile of v0, /device:TPU:0, one launch (start us, length us, event | category | flops | bytes accessed | tf_op | source)
XLA Modules:
  0.0 2963.1 jit_solution(12527253084721557049)
XLA Ops:
  14.3 43.6 %all-reduce.19 = (bf16[6912]{0:T(1024)(128)(2,1)S(1)}, bf16[3456]{0:T(1024)(128)(2,1)S(1)}, bf16[1152]{0:T(1024)(128)(2,1)}, bf16[6144]{0:T(1024)(128)(2,1)}, bf16[1152]{0:T(1024)(128)(2,1)}) all-reduce(bf16[6912]{0:T(1024)(128)(2,1)S(1)} %dynamic-update-slice, ...), channel_id=1, replica_groups=mesh['dp'=4,'row'=4,'col'=2] {'dp','row','col'}, use_global_device_ids=true, to_apply=%add | all-reduce | flops 18816 | bytes 75264
  63.0 30.1 %all-gather.16.cloned.1.call-done = bf16[32,36,3456]{2,1,0:T(8,128)(2,1)} async-done(((bf16[1,36,3456]{2,1,0:T(8,128)(2,1)}), bf16[32,36,3456]{2,1,0:T(8,128)(2,1)}) %all-gather.16.cloned.1.call-update) | async-done | bytes 7962640 | tf_op jit(solution)/shard_map/all_gather | solution.py:106
  93.1 12.6 reshape.708
  105.7 99.9 %all-gather.10.cloned.1.call-done = bf16[1152,6912]{0,1:T(8,128)(2,1)} async-done(((bf16[1152,216]{0,1:T(8,128)(2,1)}), bf16[1152,6912]{0,1:T(8,128)(2,1)}) %all-gather.10.cloned.1.call-update) | async-done | bytes 15925264 | tf_op jit(solution)/shard_map/all_gather | solution.py:104
  271.2 106.0 %all-gather.20.cloned.1.call-done = bf16[32,36,6144]{2,1,0:T(8,128)(2,1)} async-done(((bf16[1,36,6144]{2,1,0:T(8,128)(2,1)}), bf16[32,36,6144]{2,1,0:T(8,128)(2,1)}) %all-gather.20.cloned.1.call-update) | async-done | bytes 14155792 | tf_op jit(solution)/shard_map/all_gather | solution.py:110
  377.3 17.4 reshape.710
  416.2 99.9 %all-gather.12.cloned.1.call-done = bf16[4,512,2304]{2,1,0:T(8,128)(2,1)} async-done(((bf16[4,64,2304]{2,1,0:T(8,128)(2,1)}), bf16[4,512,2304]{2,1,0:T(8,128)(2,1)}) %all-gather.12.cloned.1.call-update) | async-done | bytes 9437200 | tf_op jit(solution)/shard_map/all_gather | solution.py:152
  548.0 65.6 %while.32 = (s32[]{:T(128)}, bf16[16,4,64,72]{3,2,1,0:T(8,128)(2,1)}, f32[16,4,64,1]{2,1,3,0:T(4,128)}, f32[16,4,64,1]{2,1,3,0:T(4,128)}, bf16[16,4,64,72]{3,2,1...) while((s32[]{:T(128)}, ...), condition=%wide.region_7.8_spmd.clone.clone, body=%wide.region_4.7_spmd.clone.sunk.clone | while | flops 38802944 | bytes 2380953 | solution.py:180
  650.3 12.1 multiply_reduce_fusion.8
  679.2 147.7 %while.33 = (s32[]{:T(128)}, f32[16,4,64,72]{3,2,1,0:T(8,128)}, f32[16,4,512,72]{2,3,0,1:T(8,128)}, f32[16,4,512,72]{2,3,0,1:T(8,128)}, bf16[16,4,64,72]{3,2,1,0...) while((s32[]{:T(128)}, f32[16,4,64,72]{3,2,1,0:T(8,128)}, ...), condition=%wide.region_14.15_spmd.clone.clone, body=%wide.region_12.14_spmd.clone.sunk.clone | while | flops 95854336 | bytes 6411441 | solution.py:254
  846.1 14.6 pad_maximum_fusion
  881.1 290.7 %reduce-scatter.15.cloned.1.call-done = f32[4,64,2304]{2,1,0:T(8,128)} async-done(((f32[4,512,2304]{2,1,0:T(8,128)}), f32[4,64,2304]{2,1,0:T(8,128)}) %reduce-scatter.15.cloned.1.call-update) | async-done | bytes 2359312 | tf_op jit(solution)/shard_map/reduce_scatter | solution.py:264
  1246.7 17.1 fusion.108
  1265.1 15.3 convolution_bitcast_fusion.2
  1280.5 757.5 %fusion.6 = f32[40,6144]{1,0:T(8,128)S(1)} fusion(f32[1152,6144]{1,0:T(8,128)} %convolution_bitcast_fusion.2), kind=kCustom, calls=%all-reduce-scatter.2 | all-reduce-scatter fusion | flops 7864321 | bytes 29294592
  2063.1 653.0 %fusion.112 = (f32[48,3456]{1,0:T(8,128)S(1)}, f32[48,1152]{1,0:T(8,128)S(1)}) fusion(f32[1152,3456]{1,0:T(8,128)} %convolution_bitcast_fusion.3, f32[1152,1152]{1,0:T(8,128)} %convolution_bitcast_fusion.5), kind=kCustom, calls=%all-reduce-scatter.3 | all-reduce-scatter fusion | flops 7077889 | bytes 22118400
  2717.5 35.5 %collective-permute-start.19 = (f32[4,6144]{1,0:T(4,128)S(1)}, f32[4,6144]{1,0:T(4,128)}, u32[]{:S(2)}, u32[]{:S(2)}) collective-permute-start(f32[4,6144]{1,0:T(4,128)S(1)} %slice.129), channel_id=1, source_target_pairs={{0,4},{1,5},{2,6},{3,7},{4,8},{5,9},{6,10},{7,11},{8,12},{9,13},{1... | collective-permute-start | bytes 294920
  2755.8 16.2 collective-permute-start.13
  2790.2 25.6 collective-permute-done.11
  2815.8 13.5 collective-permute-start.9
  2832.0 19.3 concatenate.24
  2885.5 14.3 concatenate.23
  2904.6 12.9 collective-permute-done.1
  2917.6 35.6 %concatenate.22 = f32[420,3456]{1,0:T(8,128)} concatenate(f32[36,3456]{1,0:T(8,128)} %collective-permute-done.7, f32[48,3456]{1,0:T(8,128)S(1)} %collective-permute-done.6, f32[48,3456]{1,0:T(8,128)} %collective-permute-done.5, f32[48,3456]{1,0:T(8,128)S(1)} %collective-permute-done.4, f32[48,3456]{1,0:T(8,128)} %collective-permute-done.3, f32[48,3456]{1,0:T(8,128)} %collective-permute-done.2, ...), dimensions={0} | concatenate | bytes 11612160
  (612 shorter events, 604.0 us)
Async XLA Ops:
  7.2 85.9 %all-gather.16.cloned.1.call-start = ((), (), s32[]{:S(2)}) async-start(), calls=%async_computation.9 | async-start | bytes 9123840 | tf_op jit(solution)/shard_map/all_gather | solution.py:106
  7.9 197.7 %all-gather.10.cloned.1.call-start = ((), (), s32[]{:S(2)}) async-start(), calls=%async_computation.4 | async-start | bytes 16422912 | tf_op jit(solution)/shard_map/all_gather | solution.py:104
  8.7 256.9 %all-gather.18.cloned.1.call-start = ((), (), s32[]{:S(2)}) async-start(), calls=%async_computation.10 | async-start | bytes 3041280 | tf_op jit(solution)/shard_map/all_gather | solution.py:108
  9.4 367.8 %all-gather.20.cloned.1.call-start = ((), (), s32[]{:S(2)}) async-start(), calls=%async_computation.11 | async-start | bytes 16220160 | tf_op jit(solution)/shard_map/all_gather | solution.py:110
  10.0 506.1 %all-gather.12.cloned.1.call-start = ((), (), s32[]{:S(2)}) async-start(), calls=%async_computation.5 | async-start | bytes 10616832 | tf_op jit(solution)/shard_map/all_gather | solution.py:152
  249.5 390.5 %all-gather.14.cloned.1.call-start = ((), (), s32[]{:S(2)}) async-start(), calls=%async_computation.6 | async-start | bytes 7299072 | tf_op jit(solution)/shard_map/all_gather | solution.py:112
  250.1 921.7 %reduce-scatter.15.cloned.1.call-start = ((), (), s32[]{:S(2)}) async-start(), calls=%async_computation.7 | async-start | bytes 21233664 | tf_op jit(solution)/shard_map/reduce_scatter | solution.py:264
  860.7 2015.4 %reduce-scatter.19.cloned.1.call-start = ((), (), s32[]{:S(2)}) async-start(), calls=%async_computation.12 | async-start | bytes 663552
  1234.9 1642.8 %all-reduce.23.cloned.1.call-start = ((), (), s32[]{:S(2)}) async-start(), calls=%async_computation.14 | async-start | bytes 182272
  1237.8 1717.3 %reduce-scatter.17.cloned.1.call-start = ((), (), s32[]{:S(2)}) async-start(), calls=%async_computation.8 | async-start | bytes 14598144 | tf_op jit(solution)/shard_map/reduce_scatter | solution.py:306
  1246.7 1708.4 %reduce-scatter.21.cloned.1.call-start = ((), (), s32[]{:S(2)}) async-start(), calls=%async_computation.13 | async-start | bytes 32845824
  2038.0 717.8 %collective-permute-start.18 = (f32[40,6144]{1,0:T(8,128)S(1)}, f32[40,6144]{1,0:T(8,128)}, u32[]{:S(2)}, u32[]{:S(2)}) collective-permute-start(f32[40,6144]{1,0:T(8,128)S(1)} %fusion.6), channel_id=1, source_target_pairs={{0,3},{1,4},{2,5},{3,6},{4,7},{5,8},{6,9},{7,10},{8,11},{9,12},{10... | collective-permute-start | bytes 2949128
  2040.4 731.7 %collective-permute-start.17 = (f32[40,6144]{1,0:T(8,128)S(1)}, f32[40,6144]{1,0:T(8,128)}, u32[]{:S(2)}, u32[]{:S(2)}) collective-permute-start(f32[40,6144]{1,0:T(8,128)S(1)} %fusion.6), channel_id=1, source_target_pairs={{0,2},{1,3},{2,4},{3,5},{4,6},{5,7},{6,8},{7,9},{8,10},{9,11},{10,... | collective-permute-start | bytes 2949128
  2048.3 727.3 %collective-permute-start.16 = (f32[40,6144]{1,0:T(8,128)S(1)}, f32[40,6144]{1,0:T(8,128)}, u32[]{:S(2)}, u32[]{:S(2)}) collective-permute-start(f32[40,6144]{1,0:T(8,128)S(1)} %fusion.6), channel_id=1, source_target_pairs={{0,1},{1,2},{2,3},{3,4},{4,5},{5,6},{6,7},{7,8},{8,9},{9,10},{10,1... | collective-permute-start | bytes 2949128
  2716.1 62.4 %collective-permute-start.15 = (f32[36,1152]{1,0:T(8,128)S(1)}, f32[36,1152]{1,0:T(8,128)S(1)}, u32[]{:S(2)}, u32[]{:S(2)}) collective-permute-start(f32[36,1152]{1,0:T(8,128)S(1)} %slice.128), channel_id=1, source_target_pairs={{0,8},{1,9},{2,10},{3,11},{4,12},{5,13},{6,14},{7,15},{8,16},{9,17... | collective-permute-start | bytes 497672
  2775.7 91.0 %collective-permute-start.6 = (f32[48,3456]{1,0:T(8,128)S(1)}, f32[48,3456]{1,0:T(8,128)S(1)}, u32[]{:S(2)}, u32[]{:S(2)}) collective-permute-start(f32[48,3456]{1,0:T(8,128)S(1)} %get-tuple-element.387), channel_id=1, source_target_pairs={{0,7},{1,8},{2,9},{3,10},{4,11},{5,12},{6,13},{7,14},{8,15},{9,16}... | collective-permute-start | bytes 1990664
  2779.2 91.3 %collective-permute-start.5 = (f32[48,3456]{1,0:T(8,128)S(1)}, f32[48,3456]{1,0:T(8,128)}, u32[]{:S(2)}, u32[]{:S(2)}) collective-permute-start(f32[48,3456]{1,0:T(8,128)S(1)} %get-tuple-element.387), channel_id=1, source_target_pairs={{0,6},{1,7},{2,8},{3,9},{4,10},{5,11},{6,12},{7,13},{8,14},{9,15},... | collective-permute-start | bytes 1990664
  2782.8 81.1 %collective-permute-start.7 = (f32[36,3456]{1,0:T(8,128)}, f32[36,3456]{1,0:T(8,128)}, u32[]{:S(2)}, u32[]{:S(2)}) collective-permute-start(f32[36,3456]{1,0:T(8,128)} %slice.127), channel_id=1, source_target_pairs={{0,8},{1,9},{2,10},{3,11},{4,12},{5,13},{6,14},{7,15},{8,16},{9,17... | collective-permute-start | bytes 1493000
  2788.8 40.5 %collective-permute-start.10 = (f32[48,1152]{1,0:T(8,128)S(1)}, f32[48,1152]{1,0:T(8,128)S(1)}, u32[]{:S(2)}, u32[]{:S(2)}) collective-permute-start(f32[48,1152]{1,0:T(8,128)S(1)} %get-tuple-element.388), channel_id=1, source_target_pairs={{0,3},{1,4},{2,5},{3,6},{4,7},{5,8},{6,9},{7,10},{8,11},{9,12},{10... | collective-permute-start | bytes 663560
  2851.3 50.2 %collective-permute-start.4 = (f32[48,3456]{1,0:T(8,128)S(1)}, f32[48,3456]{1,0:T(8,128)S(1)}, u32[]{:S(2)}, u32[]{:S(2)}) collective-permute-start(f32[48,3456]{1,0:T(8,128)S(1)} %get-tuple-element.387), channel_id=1, source_target_pairs={{0,5},{1,6},{2,7},{3,8},{4,9},{5,10},{6,11},{7,12},{8,13},{9,14},{... | collective-permute-start | bytes 1990664
  2860.9 40.6 %collective-permute-start.3 = (f32[48,3456]{1,0:T(8,128)S(1)}, f32[48,3456]{1,0:T(8,128)}, u32[]{:S(2)}, u32[]{:S(2)}) collective-permute-start(f32[48,3456]{1,0:T(8,128)S(1)} %get-tuple-element.387), channel_id=1, source_target_pairs={{0,4},{1,5},{2,6},{3,7},{4,8},{5,9},{6,10},{7,11},{8,12},{9,13},{1... | collective-permute-start | bytes 1990664
  2863.9 40.7 %collective-permute-start.2 = (f32[48,3456]{1,0:T(8,128)S(1)}, f32[48,3456]{1,0:T(8,128)}, u32[]{:S(2)}, u32[]{:S(2)}) collective-permute-start(f32[48,3456]{1,0:T(8,128)S(1)} %get-tuple-element.387), channel_id=1, source_target_pairs={{0,3},{1,4},{2,5},{3,6},{4,7},{5,8},{6,9},{7,10},{8,11},{9,12},{10... | collective-permute-start | bytes 1990664
  2866.7 50.9 %collective-permute-start.1 = (f32[48,3456]{1,0:T(8,128)S(1)}, f32[48,3456]{1,0:T(8,128)}, u32[]{:S(2)}, u32[]{:S(2)}) collective-permute-start(f32[48,3456]{1,0:T(8,128)S(1)} %get-tuple-element.387), channel_id=1, source_target_pairs={{0,2},{1,3},{2,4},{3,5},{4,6},{5,7},{6,8},{7,9},{8,10},{9,11},{10,... | collective-permute-start | bytes 1990664
  2870.5 47.0 %collective-permute-start = (f32[48,3456]{1,0:T(8,128)S(1)}, f32[48,3456]{1,0:T(8,128)}, u32[]{:S(2)}, u32[]{:S(2)}) collective-permute-start(f32[48,3456]{1,0:T(8,128)S(1)} %get-tuple-element.387), channel_id=1, source_target_pairs={{0,1},{1,2},{2,3},{3,4},{4,5},{5,6},{6,7},{7,8},{8,9},{9,10},{10,1... | collective-permute-start | bytes 1990664
  (92 other events, 2276.3 us)
Sparse Core Ops, SparseCore 0:
  10.9 82.1 all-gather.15
  95.9 109.6 all-gather.9
  208.4 57.1 all-gather.17
  268.4 108.8 all-gather.19
  379.9 136.2 all-gather.11
  518.9 70.7 all-gather.13
  860.9 310.9 reduce-scatter.14
  1235.0 62.0 reduce-scatter.18
  1305.3 159.8 all-reduce.22
  1471.6 267.3 reduce-scatter.16
  1746.1 623.3 reduce-scatter.20
where the time goes:
time: 3020 us; the launch traced here: 2960 us
  blocking collectives  1450 us (48%)
  waiting for transfers between devices  684 us (23%)
  matrix products  314 us (10%)
  local copies, waits for them, and re-layouts  284 us (9%)
  starting transfers between devices  122 us (4%)
  other arithmetic  88.2 us (3%)
    unnamed x3, blocking collectives  1450 us
    reduce_scatter x1, waiting for transfers between devices, local(): lax.psum_scatter(dkv_term, ('row', 'col'), scatter_dimension=1, tiled=True)  291 us
    unnamed x210, local copies, waits for them, and re-layouts  150 us
    unnamed x23, starting transfers between devices  122 us
    all_gather x1, waiting for transfers between devices, local(): lax.all_gather(w_gu, ('dp', 'row', 'col'), axis=0, tiled=True)  106 us
    all_gather x1, waiting for transfers between devices, local(): lax.all_gather(w_mod, ('dp', 'row', 'col'), axis=1, tiled=True)  99.9 us
    all_gather x1, waiting for transfers between devices, local(): kv_every = lax.all_gather(kv_local, ('row', 'col'), axis=1, tiled=True)  99.9 us
  transfers between devices with their start and end apart: 31, of which 10 were waited for; matrix products, arithmetic and copies ran while one was open for 61% of the time, Pallas kernels for 0%

commit v1 on v0

--- a/solution.py
+++ b/solution.py
@@ -2,7 +2,10 @@
 
 import jax
 import jax.numpy as jnp
+import numpy as np
 from jax import lax
+from jax.experimental import pallas as pl
+from jax.experimental.pallas import tpu as pltpu
 from jax.sharding import PartitionSpec as P
 
 HEADS = 16
@@ -56,7 +59,7 @@
     return (raw_grad, gain_grad)
 
 
-def local(
+def general(
     tokens,
     conditioning,
     heights,
@@ -339,6 +342,934 @@
     )
 
 
+MESH = pl.DeviceIdType.MESH
+BF = jnp.bfloat16
+F32 = jnp.float32
+LIMIT = 60 * 1024 * 1024
+D = 1152
+UNIT = 36
+PAD = 48
+TOK = 256
+GROUP = 1024
+SPLIT_Q, SPLIT_P, SPLIT_G, SPLIT_D = 384, 640, 768, 640
+ROOT = 1.0 / math.sqrt(HEAD)
+
+
+def nn(a, b):
+    return lax.dot_general(a, b, (((1,), (0,)), ((), ())), preferred_element_type=F32)
+
+
+def nt(a, b):
+    return lax.dot_general(a, b, (((1,), (1,)), ((), ())), preferred_element_type=F32)
+
+
+def tn(a, b):
+    return lax.dot_general(a, b, (((0,), (0,)), ((), ())), preferred_element_type=F32)
+
+
+def width_order():
+    xx, zh, yy, zl, cc, jj = np.indices((2, 2, 2, 2, 2, UNIT)).reshape(6, -1)
+    return ((((xx * 2 + cc) * 2 + zh) * 2 + zl) * 2 + yy) * UNIT + jj
+
+
+def constants():
+    perm = np.zeros((D, D), np.float32)
+    perm[width_order(), np.arange(D)] = 1.0
+    spread = np.zeros((864, 1536), np.float32)
+    tt, hh, yy, jj = np.indices((3, 4, 2, UNIT)).reshape(4, -1)
+    spread[tt * 288 + hh * 72 + yy * 36 + jj, tt * 512 + hh * 128 + yy * 64 + jj] = 1.0
+    pick = np.zeros((144, 192), np.float32)
+    kk, jj = np.indices((4, UNIT)).reshape(2, -1)
+    pick[kk * 36 + jj, kk * 48 + jj] = 1.0
+    spot = np.arange(512)
+    row = spot // 128 * 4 + spot // 16 % 4
+    col = spot // 64 % 2 * 16 + spot % 16
+    lane = np.arange(128)
+    part = lane % 64
+    freq = np.exp(-math.log(10000.0) * 2.0 * (part // 2) / 36.0)
+    place = np.where(lane[None, :] >= 64, col[:, None], row[:, None]).astype(np.float64)
+    angle = place * freq[None, :]
+    live = part < UNIT
+    cos = np.where(live, np.cos(angle), 0.0)
+    sin = np.where(live, np.sin(angle), 0.0)
+    even = lane % 2 == 0
+    tabs = np.stack([cos, np.where(even, -sin, 0.0), np.where(even, 0.0, sin)]).astype(np.float32)
+    return (
+        jnp.asarray(perm, BF),
+        jnp.asarray(spread, BF),
+        jnp.asarray(pick, BF),
+        jnp.asarray(tabs, F32),
+        row,
+        col,
+    )
+
+
+class Place:
+    def __init__(self):
+        dp = lax.axis_index("dp")
+        self.z = lax.axis_index("row")
+        self.y = lax.axis_index("col")
+        self.x = dp // 2
+        self.c = dp % 2
+        self.zh = self.z // 2
+        self.zl = self.z % 2
+        self.m = self.zl * 2 + self.c
+        self.dp = dp
+
+    def mate(self, r):
+        c = 1 - self.c if r % 2 else self.c
+        zl = 1 - self.zl if r // 2 else self.zl
+        return zl * 2 + c, (self.x * 2 + c, self.zh * 2 + zl, self.y)
+
+    def xpeer(self):
+        return ((1 - self.x) * 2 + self.c, self.z, self.y)
+
+    def ypeer(self):
+        return (self.dp, self.z, 1 - self.y)
+
+    def zpeer(self):
+        return (self.dp, (1 - self.zh) * 2 + self.zl, self.y)
+
+    def item_home(self, j):
+        return (self.x * 2 + self.zh, j, self.c)
+
+    def item_source(self, blk):
+        return (self.x * 2 + self.y, self.c * 2 + blk // 2, blk % 2)
+
+    def is_me(self, dev):
+        return (dev[0] == self.dp) & (dev[1] == self.z) & (dev[2] == self.y)
+
+
+class Link:
+    def __init__(self, here, ssem, rsem):
+        self.here, self.ssem, self.rsem, self.n, self.open = here, ssem, rsem, 0, []
+
+    def greet(self, items):
+        here = self.here
+        bar = pltpu.get_barrier_semaphore()
+        devs = [here.mate(r)[1] for r in (1, 2, 3)]
+        devs += [here.xpeer(), here.ypeer(), here.zpeer()]
+        for d in devs:
+            pl.semaphore_signal(bar, inc=1, device_id=d, device_id_type=MESH)
+        total = len(devs)
+        if items:
+            for d in [here.item_home(j) for j in range(4)] + [here.item_source(j) for j in range(4)]:
+
+
+                @pl.when(jnp.logical_not(here.is_me(d)))
+                def _():
+                    pl.semaphore_signal(bar, inc=1, device_id=d, device_id_type=MESH)
+
+            far = (here.zh - here.c) * (here.zh - here.c)
+            off = (here.y - here.c) * (here.y - here.c)
+            total += 8 - 2 * (1 - far) * (1 - off)
+        pl.semaphore_wait(bar, total)
+
+    def send(self, src, dst, dev):
+        k = self.n
+        self.n += 1
+        copy = pltpu.make_async_remote_copy(
+            src_ref=src,
+            dst_ref=dst,
+            send_sem=self.ssem.at[k],
+            recv_sem=self.rsem.at[k],
+            device_id=dev,
+            device_id_type=MESH,
+        )
+        copy.start()
+        self.open.append(copy)
+        return copy
+
+    def scatter(self, src_of, dst, dev_of, slot):
+        base = self.n
+        self.n += 4
+        here = self.here
+        copies = []
+        for j in range(4):
+            dev = dev_of(j)
+            mine = here.is_me(dev)
+            remote = pltpu.make_async_remote_copy(
+                src_ref=src_of(j),
+                dst_ref=dst,
+                send_sem=self.ssem.at[base + j],
+                recv_sem=self.rsem.at[base + slot],
+                device_id=dev,
+                device_id_type=MESH,
+            )
+            local_copy = pltpu.make_async_copy(src_of(j), dst, self.rsem.at[base + slot])
+
+            @pl.when(mine)
+            def _():
+                local_copy.start()
+
+            @pl.when(jnp.logical_not(mine))
+            def _():
+                remote.start()
+
+            copies.append((mine, remote))
+
+        def wait_send():
+            for mine, remote in copies:
+
+                @pl.when(jnp.logical_not(mine))
+                def _():
+                    remote.wait_send()
+
+        def wait_recv(src, dst_of):
+            for j in range(4):
+                pltpu.make_async_copy(src, dst_of(j), self.rsem.at[base + j]).wait()
+
+        return wait_send, wait_recv
+
+    def finish(self):
+        for copy in self.open:
+            copy.wait_send()
+        self.open = []
+
+
+def norm_rows(x):
+    mean = jnp.sum(x, -1, keepdims=True) * (1.0 / D)
+    cent = x - mean
+    var = jnp.sum(cent * cent, -1, keepdims=True) * (1.0 / D)
+    recip = lax.rsqrt(var + EPSILON)
+    return cent * recip, recip
+
+
+def norm_rows_back(g, y, recip):
+    mg = jnp.sum(g, -1, keepdims=True) * (1.0 / D)
+    mgy = jnp.sum(g * y, -1, keepdims=True) * (1.0 / D)
+    return recip * (g - mg - y * mgy)
+
+
+def at(i, n):
+    return pl.ds(pl.multiple_of(i * n, n), n)
+
+
+class Gather:
+    def __init__(self, link, ref, rows, split):
+        self.link, self.ref, self.rows, self.split = link, ref, rows, split
+
+    def cut(self, i, j, k, cols):
+        return self.ref.at[i, j, k, pl.ds(0, self.rows), cols]
+
+    def hop1(self):
+        h = self.link.here
+        part = self.cut(h.x, h.zh, h.y, slice(None))
+        self.a = self.link.send(part, part, h.zpeer())
+
+    def hop2(self):
+        h = self.link.here
+        self.a.wait_recv()
+        pa = self.cut(h.x, slice(None), h.y, pl.ds(0, self.split))
+        pb = self.cut(h.x, slice(None), h.y, pl.ds(self.split, self.ref.shape[-1] - self.split))
+        self.a = self.link.send(pa, pa, h.xpeer())
+        self.b = self.link.send(pb, pb, h.ypeer())
+
+    def hop3(self):
+        h = self.link.here
+        self.a.wait_recv()
+        self.b.wait_recv()
+        pa = self.cut(slice(None), slice(None), h.y, pl.ds(0, self.split))
+        pb = self.cut(
+            h.x, slice(None), slice(None), pl.ds(self.split, self.ref.shape[-1] - self.split)
+        )
+        self.a = self.link.send(pa, pa, h.ypeer())
+        self.b = self.link.send(pb, pb, h.xpeer())
+
+    def done(self):
+        self.a.wait_recv()
+        self.b.wait_recv()
+
+
+class Reduce:
+    def __init__(self, link, ref, bufs, split):
+        self.link, self.ref, self.split = link, ref, split
+        self.cols = ref.shape[-1]
+        self.r1a, self.r1b, self.r2a, self.r2b, self.r3a, self.r3b = bufs
+
+    @staticmethod
+    def buffers(rows, cols, split):
+        rest = cols - split
+        return [
+            pltpu.VMEM((2, 2, rows, split), BF),
+            pltpu.VMEM((2, 2, rows, rest), BF),
+            pltpu.VMEM((2, rows, split), BF),
+            pltpu.VMEM((2, rows, rest), BF),
+            pltpu.VMEM((rows, split), BF),
+            pltpu.VMEM((rows, rest), BF),
+        ]
+
+    def hop1(self):
+        h = self.link.here
+        ca, cb = pl.ds(0, self.split), pl.ds(self.split, self.cols - self.split)
+        self.a = self.link.send(self.ref.at[1 - h.x, :, :, :, ca], self.r1a, h.xpeer())
+        self.b = self.link.send(self.ref.at[:, :, 1 - h.y, :, cb], self.r1b, h.ypeer())
+
+    def hop2(self):
+        h = self.link.here
+        ca, cb = pl.ds(0, self.split), pl.ds(self.split, self.cols - self.split)
+        self.a.wait_recv()
+        self.b.wait_recv()
+
+        def add(i, carry):
+            u, v = i // 2, i % 2
+            own = self.ref[h.x, u, v, :, ca].astype(F32)
+            self.r1a[u, v] = (self.r1a[u, v].astype(F32) + own).astype(BF)
+            own = self.ref[u, v, h.y, :, cb].astype(F32)
+            self.r1b[u, v] = (self.r1b[u, v].astype(F32) + own).astype(BF)
+            return carry
+
+        lax.fori_loop(0, 4, add, 0)
+        self.a = self.link.send(self.r1a.at[:, 1 - h.y], self.r2a, h.ypeer())
+        self.b = self.link.send(self.r1b.at[1 - h.x], self.r2b, h.xpeer())
+
+    def hop3(self):
+        h = self.link.here
+        self.a.wait_recv()
+        self.b.wait_recv()
+
+        def add(u, carry):
+            own = self.r1a[u, h.y].astype(F32)
+            self.r2a[u] = (self.r2a[u].astype(F32) + own).astype(BF)
+            own = self.r1b[h.x, u].astype(F32)
+            self.r2b[u] = (self.r2b[u].astype(F32) + own).astype(BF)
+            return carry
+
+        lax.fori_loop(0, 2, add, 0)
+        self.a = self.link.send(self.r2a.at[1 - h.zh], self.r3a, h.zpeer())
+        self.b = self.link.send(self.r2b.at[1 - h.zh], self.r3b, h.zpeer())
+
+    def done(self):
+        h = self.link.here
+        self.a.wait_recv()
+        self.b.wait_recv()
+        left = self.r2a[h.zh].astype(F32) + self.r3a[...].astype(F32)
+        right = self.r2b[h.zh].astype(F32) + self.r3b[...].astype(F32)
+        return left.astype(BF), right.astype(BF)
+
+
+def all_rows(link, ref):
+    here = link.here
+    own = ref.at[at(here.m, TOK)]
+    return {r: link.send(own, own, here.mate(r)[1]) for r in (2, 3, 1)}
+
+
+def turn(v, cos, sina, sinb):
+    return v * cos + pltpu.roll(v, 127, 1) * sina + pltpu.roll(v, 1, 1) * sinb
+
+
+def turn_back(d, cos, sina, sinb):
+    return d * cos - pltpu.roll(d, 127, 1) * sina - pltpu.roll(d, 1, 1) * sinb
+
+
+def kernel_a(
+    tok_in, cot_in, wq_in, wg_in, wp_in, wd_in, perm, spread, pick, tabs, gains, modv, bq, bp, maskb, valid,
+    wq, wp, wg, wd, ha, rawq, rawk, qr, kr, vv, att, hm, dmlp, tokp, og, attn_out,
+    s0q, s0g, tokr, cotr, wqe, psend, precv, pown, ssem, rsem, lsem,
+):
+    here = Place()
+    link = Link(here, ssem, rsem)
+    link.greet(True)
+    m = here.m
+    slot = here.zl * 2 + here.y
+    rows_in = at(slot, 64)
+    tok_sent, tok_got = link.scatter(lambda j: tok_in.at[j], tokr.at[rows_in], here.item_home, slot)
+    sq, sg = {}, {}
+    for r in (2, 3, 1):
+        k, dev = here.mate(r)
+        sq[r] = link.send(wq_in.at[k], s0q.at[m], dev)
+    own_q = pltpu.make_async_copy(wq_in.at[m], s0q.at[m], lsem.at[0])
+    own_q.start()
+    for r in (2, 3, 1):
+        k, dev = here.mate(r)
+        sg[r] = link.send(wg_in.at[k], s0g.at[m], dev)
+    own_g = pltpu.make_async_copy(wg_in.at[m], s0g.at[m], lsem.at[1])
+    own_g.start()
+
+    gq = Gather(link, wq, 144, SPLIT_Q)
+    gp = Gather(link, wp, PAD, SPLIT_P)
+    gg = Gather(link, wg, 144, SPLIT_G)
+    gd = Gather(link, wd, 96, SPLIT_D)
+
+    own_q.wait()
+    for r in (1, 2, 3):
+        sq[r].wait_recv()
+    wq[here.x, here.zh, here.y] = nn(pick[...], s0q[...].reshape(192, 864)).astype(BF)
+    gq.hop1()
+    wp[:, :, :, PAD:64, :] = jnp.zeros((2, 2, 2, 64 - PAD, D), BF)
+    wp[here.x, here.zh, here.y, 0:PAD, :] = nn(wp_in[...], perm[...]).astype(BF)
+    gp.hop1()
+    own_g.wait()
+    for r in (1, 2, 3):
+        sg[r].wait_recv()
+    wg[here.x, here.zh, here.y] = nn(pick[...], s0g[...].reshape(192, 1536)).astype(BF)
+    tok_got(tok_in.at[0], lambda j: tokr.at[pl.ds(j * 64, 64)])
+    gg.hop1()
+    wd[here.x, here.zh, here.y] = nn(wd_in[...], perm[...]).astype(BF)
+    gd.hop1()
+
+    tokp[...] = nn(tokr[...], perm[...]).astype(BF)
+
+    def first_norm(i, carry):
+        n, _ = norm_rows(tokp[at(i, 32), :].astype(F32))
+        h = n * (1.0 + modv[1:2, :]) + modv[0:1, :]
+        ha[pl.ds(pl.multiple_of(m * TOK + i * 32, 32), 32), :] = h.astype(BF)
+        return carry
+
+    lax.fori_loop(0, 8, first_norm, 0)
+    ha_sent = all_rows(link, ha)
+    cot_sent, cot_got = link.scatter(lambda j: cot_in.at[j], cotr.at[rows_in], here.item_home, slot)
+    gq.hop2()
+    gp.hop2()
+    gq.hop3()
+    gp.hop3()
+    for r in (1, 2, 3):
+        ha_sent[r].wait_recv()
+    gq.done()
+
+    def widen(i, carry):
+        part = wq[i // 2, i % 2].reshape(288, 864)
+        wqe[at(i, 288), :] = nn(part, spread[...]).astype(BF)
+        return carry
+
+    lax.fori_loop(0, 4, widen, 0)
+
+    def project(b, carry):
+        acc = nn(ha[at(b, TOK), :], wqe[...]) + bq[...]
+        item, half = b // 2, at(b % 2, TOK)
+        cos, sina, sinb = tabs[0, half, :], tabs[1, half, :], tabs[2, half, :]
+        for h in range(4):
+            p = item * 4 + h
+            for t, raw, rot in ((0, rawq, qr), (1, rawk, kr)):
+                v = acc[:, t * 512 + h * 128 : t * 512 + h * 128 + 128]
+                recip = lax.rsqrt(jnp.sum(v * v, -1, keepdims=True) * (1.0 / HEAD) + EPSILON)
+                raw[p, half, :] = v
+                n = v * recip * gains[t : t + 1, :]
+                rot[p, half, :] = turn(n, cos, sina, sinb).astype(BF)
+            vv[p, half, :] = acc[:, 1024 + h * 128 : 1152 + h * 128].astype(BF)
+        return carry
+
+    lax.fori_loop(0, 4, project, 0)
+    gg.hop2()
+    gd.hop2()
+
+    def attend(p, carry):
+        item = p // 4
+        lanes = at(p % 4, 128)
+        for half in range(2):
+            rows = pl.ds(half * TOK, TOK)
+            s = nt(qr[p, rows, :], kr[p]) * ROOT + maskb[item]
+            top = jnp.max(s, -1, keepdims=True)
+            e = jnp.exp(s - top)
+            pr = (e / jnp.sum(e, -1, keepdims=True)).astype(BF)
+            out_rows = pl.ds(pl.multiple_of(item * 512 + half * TOK, TOK), TOK)
+            att[out_rows, lanes] = nn(pr, vv[p]).astype(BF)
+        return carry
+
+    lax.fori_loop(0, 4, attend, 0)
+    gg.hop3()
+    gd.hop3()
+    lax.fori_loop(4, 8, attend, 0)
+    gp.done()
+    wpf = wp[...].reshape(512, D)
+    sent = {}
+    for r in (2, 3, 1):
+        k, dev = here.mate(r)
+        psend[r - 1] = nn(att[at(k, TOK), :], wpf).astype(BF)
+        sent[r] = link.send(psend.at[r - 1], precv.at[r - 1], dev)
+    pown[...] = nn(att[at(m, TOK), :], wpf)
+    cot_got(cot_in.at[0], lambda j: cotr.at[pl.ds(j * 64, 64)])
+    og[...] = (nn(cotr[...], perm[...]) * valid[...]).astype(BF)
+
+    def scale_grad(i, carry):
+        g = og[at(i, 32), :].astype(F32) * modv[5:6, :]
+        dmlp[pl.ds(pl.multiple_of(m * TOK + i * 32, 32), 32), :] = g.astype(BF)
+        return carry
+
+    lax.fori_loop(0, 8, scale_grad, 0)
+    for r in (1, 2, 3):
+        sent[r].wait_recv()
+
+    def second_norm(i, carry):
+        rows = at(i, 32)
+        a = pown[rows, :] + bp[...]
+        for r in range(3):
+            a += precv[r, rows, :].astype(F32)
+        attn_out[rows, :] = a
+        n, _ = norm_rows(tokp[rows, :].astype(F32) + modv[2:3, :] * a)
+        h = n * (1.0 + modv[4:5, :]) + modv[3:4, :]
+        hm[pl.ds(pl.multiple_of(m * TOK + i * 32, 32), 32), :] = h.astype(BF)
+        return carry
+
+    lax.fori_loop(0, 8, second_norm, 0)
+    hm_sent = all_rows(link, hm)
+    dm_sent = all_rows(link, dmlp)
+    for r in (1, 2, 3):
+        hm_sent[r].wait_recv()
+        dm_sent[r].wait_recv()
+    gg.done()
+    gd.done()
+    link.finish()
+    tok_sent()
+    cot_sent()
+
+
+def store_tiles(val, ref, base, piece, keep):
+    block = ref.shape[3] if keep is None else piece
+    for q in range(val.shape[0] // piece):
+        row = base + q * piece
+        f, off = row // block, row % block
+        n = piece if keep is None else keep
+        ref[f // 4, f // 2 % 2, f % 2, off : off + n, :] = val[q * piece : q * piece + n, :].astype(BF)
+
+
+def kernel_b(
+    wg, wd, hm, dmlp, tokp, og, attn_out, modv, bg, bd, perm, valid,
+    dwg, dwd, dattn, dmid, bout, small, dbg,
+    gu, coef, hid, hsend, hrecv, hown, msend, mrecv, mown, bo, ssem, rsem,
+):
+    here = Place()
+    link = Link(here, ssem, rsem)
+    link.greet(True)
+    m = here.m
+    wgf = wg[...].reshape(D, 1536)
+    wdf = wd[...].reshape(768, D)
+    small[...] = jnp.zeros_like(small)
+    dbg[...] = jnp.zeros_like(dbg)
+
+    def mlp(k):
+        gu[...] = nn(hm[at(k, TOK), :], wgf) + bg[...]
+
+        def acts(i, carry):
+            rows = at(i, 32)
+            out = pl.ds(pl.multiple_of(k * TOK + i * 32, 32), 32)
+            g, u = gu[rows, 0:768], gu[rows, 768:1536]
+            sig = jax.nn.sigmoid(g)
+            act = g * sig
+            hid[out, :] = (act * u).astype(BF)
+            gu[rows, 0:768] = u * sig * (1.0 + g * (1.0 - sig))
+            gu[rows, 768:1536] = act
+            return carry
+
+        lax.fori_loop(0, 8, acts, 0)
+        dh = nt(dmlp[at(k, TOK), :], wdf)
+        out = at(k, TOK)
+        coef[out, 0:768] = (gu[:, 0:768] * dh).astype(BF)
+        coef[out, 768:1536] = (gu[:, 768:1536] * dh).astype(BF)
+        dbg[0:1, :] += jnp.sum(coef[out, :].astype(F32), 0, keepdims=True)
+
+    hs, ms = {}, {}
+    for r in (2, 3, 1):
+        k, dev = here.mate(r)
+        mlp(k)
+        hsend[r - 1] = nt(coef[at(k, TOK), :], wgf).astype(BF)
+        hs[r] = link.send(hsend.at[r - 1], hrecv.at[r - 1], dev)
+    mlp(m)
+    hown[...] = nt(coef[at(m, TOK), :], wgf)
+    for r in (2, 3, 1):
+        k, dev = here.mate(r)
+        msend[r - 1] = nn(hid[at(k, TOK), :], wdf).astype(BF)
+        ms[r] = link.send(msend.at[r - 1], mrecv.at[r - 1], dev)
+    mown[...] = nn(hid[at(m, TOK), :], wdf)
+    for r in (1, 2, 3):
+        hs[r].wait_recv()
+
+    def mid_back(i, carry):
+        rows = at(i, 32)
+        d = hown[rows, :]
+        for r in range(3):
+            d += hrecv[r, rows, :].astype(F32)
+        a = attn_out[rows, :]
+        n, recip = norm_rows(tokp[rows, :].astype(F32) + modv[2:3, :] * a)
+        small[1:2, :] += jnp.sum(d, 0, keepdims=True)
+        small[2:3, :] += jnp.sum(d * n, 0, keepdims=True)
+        g = og[rows, :].astype(F32) + norm_rows_back(d * (1.0 + modv[4:5, :]), n, recip)
+        dmid[rows, :] = g
+        small[3:4, :] += jnp.sum(g * a, 0, keepdims=True)
+        low = (modv[2:3, :] * g).astype(BF)
+        dattn[pl.ds(pl.multiple_of(m * TOK + i * 32, 32), 32), :] = low
+        small[5:6, :] += jnp.sum(low.astype(F32), 0, keepdims=True)
+        return carry
+
+    lax.fori_loop(0, 8, mid_back, 0)
+    da = all_rows(link, dattn)
+    for i in range(3):
+        store_tiles(tn(hm[:, i * 384 : i * 384 + 384], coef[...]), dwg, i * 384, 48, None)
+    for i in range(2):
+        store_tiles(tn(hid[:, i * 384 : i * 384 + 384], dmlp[...]), dwd, i * 384, 96, None)
+    for r in (1, 2, 3):
+        ms[r].wait_recv()
+
+    def finish_out(i, carry):
+        rows = at(i, 32)
+        o = mown[rows, :] + bd[...]
+        for r in range(3):
+            o += mrecv[r, rows, :].astype(F32)
+        g = og[rows, :].astype(F32)
+        small[0:1, :] += jnp.sum(g * o, 0, keepdims=True)
+        mine = dmlp[pl.ds(pl.multiple_of(m * TOK + i * 32, 32), 32), :]
+        small[4:5, :] += jnp.sum(mine.astype(F32), 0, keepdims=True)
+        mid = tokp[rows, :].astype(F32) + modv[2:3, :] * attn_out[rows, :]
+        bo[rows, :] = ((mid + modv[5:6, :] * o) * valid[rows, :]).astype(BF)
+        return carry
+
+    lax.fori_loop(0, 8, finish_out, 0)
+    bo[...] = nt(bo[...], perm[...]).astype(BF)
+    sent, got = link.scatter(
+        lambda j: bo.at[pl.ds(j * 64, 64)], bout.at[here.z], here.item_source, here.z
+    )
+    for r in (1, 2, 3):
+        da[r].wait_recv()
+    got(bo.at[pl.ds(0, 64)], lambda j: bout.at[j])
+    link.finish()
+    sent()
+
+
+def kernel_c(
+    dwg, dwd, dattn, att, wp, wq, ha, rawq, rawk, qr, kr, vv, maskb, dmid, tokp, modv, gains, tabs, perm, spread, pick,
+    dtok, fq, fg, fp, fd, small, dbq, dgain,
+    dwq, dwp, datt, de, dc, tsend, trecv, town, to, eq, eg,
+    g1a, g1b, g2a, g2b, g3a, g3b, d1a, d1b, d2a, d2b, d3a, d3b,
+    q1a, q1b, q2a, q2b, q3a, q3b, p1a, p1b, p2a, p2b, p3a, p3b, ssem, rsem,
+):
+    here = Place()
+    link = Link(here, ssem, rsem)
+    link.greet(True)
+    m = here.m
+    rg = Reduce(link, dwg, (g1a, g1b, g2a, g2b, g3a, g3b), SPLIT_G)
+    rd = Reduce(link, dwd, (d1a, d1b, d2a, d2b, d3a, d3b), SPLIT_D)
+    rq = Reduce(link, dwq, (q1a, q1b, q2a, q2b, q3a, q3b), SPLIT_Q)
+    rp = Reduce(link, dwp, (p1a, p1b, p2a, p2b, p3a, p3b), SPLIT_P)
+    rg.hop1()
+    rd.hop1()
+    small[...] = jnp.zeros_like(small)
+    dgain[...] = jnp.zeros_like(dgain)
+    dbq[...] = jnp.zeros_like(dbq)
+    wpf = wp[...].reshape(512, D)
+
+    def back_proj(b, carry):
+        datt[at(b, TOK), :] = nt(dattn[at(b, TOK), :], wpf).astype(BF)
+        return carry
+
+    lax.fori_loop(0, 4, back_proj, 0)
+    store_tiles(tn(att[...], dattn[...]), dwp, 0, 64, PAD)
+    rp.hop1()
+
+    def attend_back(p, carry):
+        item = p // 4
+        lanes = at(p % 4, 128)
+        rows_all = at(item, 512)
+        dk = jnp.zeros((512, 128), F32)
+        dv = jnp.zeros((512, 128), F32)
+
+        def head_back_store(d, raw_ref, row, t, rows, out_rows):
+            cos, sina, sinb = tabs[0, rows, :], tabs[1, rows, :], tabs[2, rows, :]
+            raw = raw_ref[p, rows, :]
+            recip = lax.rsqrt(jnp.sum(raw * raw, -1, keepdims=True) * (1.0 / HEAD) + EPSILON)
+            dn = turn_back(d, cos, sina, sinb)
+            dgain[t : t + 1, :] += jnp.sum(dn * raw * recip, 0, keepdims=True)
+            u = dn * gains[t : t + 1, :]
+            mean = jnp.sum(u * raw, -1, keepdims=True) * (1.0 / HEAD)
+            res = recip * u - raw * (recip * recip * recip * mean)
+            de[out_rows, at(t * 4 + p % 4, 128)] = res.astype(BF)
+
+        for half in range(2):
+            rows = pl.ds(half * TOK, TOK)
+            out_rows = pl.ds(pl.multiple_of(item * 512 + half * TOK, TOK), TOK)
+            do = datt[out_rows, lanes]
+            s = nt(qr[p, rows, :], kr[p]) * ROOT + maskb[item]
+            e = jnp.exp(s - jnp.max(s, -1, keepdims=True))
+            pf = e / jnp.sum(e, -1, keepdims=True)
+            pr = pf.astype(BF)
+            dp = nt(do, vv[p])
+            delta = jnp.sum(pf * dp, -1, keepdims=True)
+            ds = (pf * (dp - delta)).astype(BF)
+            dq = nn(ds, kr[p]) * ROOT
+            dk += tn(ds, qr[p, rows, :])
+            dv += tn(pr, do)
+            head_back_store(dq, rawq, None, 0, rows, out_rows)
+        dk = dk * ROOT
+        for half in range(2):
+            rows = pl.ds(half * TOK, TOK)
+            out_rows = pl.ds(pl.multiple_of(item * 512 + half * TOK, TOK), TOK)
+            head_back_store(dk[half * TOK : half * TOK + TOK], rawk, None, 1, rows, out_rows)
+        de[rows_all, at(8 + p % 4, 128)] = dv.astype(BF)
+        return carry
+
+    lax.fori_loop(0, 4, attend_back, 0)
+    rg.hop2()
+    rd.hop2()
+    rp.hop2()
+    lax.fori_loop(4, 8, attend_back, 0)
+    rg.hop3()
+    rd.hop3()
+    rp.hop3()
+
+    def squeeze(b, carry):
+        v = de[at(b, TOK), :]
+        dbq[0:1, :] += jnp.sum(v.astype(F32), 0, keepdims=True)
+        dc[at(b, TOK), :] = nt(v, spread[...]).astype(BF)
+        return carry
+
+    lax.fori_loop(0, 4, squeeze, 0)
+    wqf = wq[...].reshape(D, 864)
+    ts = {}
+    for r in (2, 3, 1):
+        k, dev = here.mate(r)
+        tsend[r - 1] = nt(dc[at(k, TOK), :], wqf).astype(BF)
+        ts[r] = link.send(tsend.at[r - 1], trecv.at[r - 1], dev)
+    town[...] = nt(dc[at(m, TOK), :], wqf)
+    for i in range(3):
+        store_tiles(tn(ha[:, i * 384 : i * 384 + 384], dc[...]), dwq, i * 384, 48, None)
+    rq.hop1()
+    for r in (1, 2, 3):
+        ts[r].wait_recv()
+
+    def first_back(i, carry):
+        rows = at(i, 32)
+        d = town[rows, :]
+        for r in range(3):
+            d += trecv[r, rows, :].astype(F32)
+        n, recip = norm_rows(tokp[rows, :].astype(F32))
+        small[0:1, :] += jnp.sum(d, 0, keepdims=True)
+        small[1:2, :] += jnp.sum(d * n, 0, keepdims=True)
+        g = dmid[rows, :] + norm_rows_back(d * (1.0 + modv[1:2, :]), n, recip)
+        to[rows, :] = g.astype(BF)
+        return carry
+
+    lax.fori_loop(0, 8, first_back, 0)
+    to[...] = nt(to[...], perm[...]).astype(BF)
+    sent, got = link.scatter(
+        lambda j: to.at[pl.ds(j * 64, 64)], dtok.at[here.z], here.item_source, here.z
+    )
+    rq.hop2()
+
+    def hand_out(red, exp, out, cols):
+        left, right = red.done()
+        exp[:, :, 0 : red.split] = tn(pick[...], left).astype(BF).reshape(4, PAD, red.split)
+        exp[:, :, red.split : cols] = tn(pick[...], right).astype(BF).reshape(4, PAD, cols - red.split)
+        got_it = {}
+        for r in (2, 3, 1):
+            k, dev = here.mate(r)
+            got_it[r] = link.send(exp.at[k], out.at[m], dev)
+        out[m] = exp[m]
+        return got_it
+
+    def plain(red, out):
+        left, right = red.done()
+        out[...] = nt(left, perm[:, 0 : red.split]) + nt(right, perm[:, red.split : D])
+
+    og_ = hand_out(rg, eg, fg, 1536)
+    plain(rd, fd)
+    plain(rp, fp)
+    rq.hop3()
+    oq_ = hand_out(rq, eq, fq, 864)
+    for r in (1, 2, 3):
+        og_[r].wait_recv()
+        oq_[r].wait_recv()
+    got(to.at[pl.ds(0, 64)], lambda j: dtok.at[j])
+    link.finish()
+    sent()
+
+
+def call(kernel, ident, outs, scratch, args, hbm=(), sems=64):
+    vm = pl.BlockSpec(memory_space=pltpu.VMEM)
+    hb = pl.BlockSpec(memory_space=pltpu.HBM)
+    return pl.pallas_call(
+        kernel,
+        out_shape=[jax.ShapeDtypeStruct(s, t) for s, t in outs],
+        in_specs=[hb if i in hbm else vm for i in range(len(args))],
+        out_specs=[vm] * len(outs),
+        scratch_shapes=scratch + [pltpu.SemaphoreType.DMA((sems,)), pltpu.SemaphoreType.DMA((sems,))]
+        + ([pltpu.SemaphoreType.DMA((2,))] if hbm else []),
+        compiler_params=pltpu.CompilerParams(
+            collective_id=ident, has_side_effects=True, vmem_limit_bytes=LIMIT
+        ),
+    )(*args)
+
+
+def to_order(v):
+    lead = v.shape[:-1]
+    n = len(lead)
+    v = v.reshape(lead + (2, 2, 2, 2, 2, UNIT))
+    return v.transpose(tuple(range(n)) + tuple(n + i for i in (0, 2, 4, 3, 1, 5))).reshape(lead + (D,))
+
+
+def from_order(v):
+    lead = v.shape[:-1]
+    n = len(lead)
+    v = v.reshape(lead + (2, 2, 2, 2, 2, UNIT))
+    return v.transpose(tuple(range(n)) + tuple(n + i for i in (0, 4, 1, 3, 2, 5))).reshape(lead + (D,))
+
+
+def local(
+    tokens, conditioning, heights, widths, cotangent, w_mod, b_mod, w_qkv, b_qkv, query_gain, key_gain,
+    w_proj, b_proj, w_gu, b_gu, w_down, b_down,
+):
+    args = (
+        tokens, conditioning, heights, widths, cotangent, w_mod, b_mod, w_qkv, b_qkv, query_gain, key_gain,
+        w_proj, b_proj, w_gu, b_gu, w_down, b_down,
+    )
+    sizes = tuple(lax.axis_size(a) for a in ("dp", "row", "col"))
+    if sizes != (4, 4, 2) or tokens.shape != (4, 4, 16, D):
+        return general(*args)
+    every = ("dp", "row", "col")
+    perm, spread, pick, tabs, row_of, col_of = constants()
+    dp, z, y = (lax.axis_index(a) for a in every)
+    x, c, zh, zl = dp // 2, dp % 2, z // 2, z % 2
+    pack = jnp.concatenate(
+        [conditioning.reshape(-1), heights.astype(BF), widths.astype(BF)]
+    )
+    pack = lax.all_gather(pack, "dp", axis=0)
+    cond = pack[:, : 4 * D].reshape(16, D).astype(F32)
+    tall = pack[:, 4 * D : 4 * D + 4].reshape(16).astype(jnp.int32)
+    wide = pack[:, 4 * D + 4 :].reshape(16).astype(jnp.int32)
+    act = (cond * jax.nn.sigmoid(cond)).astype(BF)
+    part = jnp.dot(act, w_mod, preferred_element_type=F32) + b_mod.astype(F32)
+    pack = jnp.concatenate([part.reshape(-1)] + [b.astype(F32) for b in (b_qkv, b_proj, b_gu, b_down)])
+    pack = lax.all_gather(pack, every, axis=0)
+    item = (2 * x + y) * 4 + z
+    modv = lax.dynamic_index_in_dim(pack[:, :3456].reshape(32, 16, 216), item, 1, False)
+    modv = to_order(modv.reshape(6, D))
+    modv = jnp.concatenate([modv, jnp.zeros((2, D), F32)])
+    own = lambda v: lax.dynamic_index_in_dim(
+        lax.dynamic_index_in_dim(v, c, 2, False), zl, 3, False
+    )
+    bq = own(pack[:, 3456:3564].reshape(3, 2, 2, 2, 2, 2, UNIT))
+    bq = jnp.pad(bq, ((0, 0),) * 4 + ((0, 64 - UNIT),)).reshape(1, 1536)
+    bp = to_order(pack[:, 3564:3600].reshape(1, D))
+    bg = own(pack[:, 3600:3792].reshape(2, 2, 2, 2, 2, 2, 96)).reshape(1, 1536)
+    bd = to_order(pack[:, 3792:3828].reshape(1, D))
+    pair = (2 * x + y) * 4 + 2 * zh + jnp.arange(2)
+    row_of, col_of = jnp.asarray(row_of), jnp.asarray(col_of)
+    live = (row_of[None] < tall[pair][:, None]) & (col_of[None] < wide[pair][:, None])
+    maskb = jnp.where(live, 0.0, MASKED).astype(F32).reshape(2, 1, 512)
+    valid = lax.dynamic_slice(live[zl].astype(F32), (c * TOK,), (TOK,)).reshape(TOK, 1)
+    gains = jnp.pad(
+        jnp.stack([query_gain, key_gain]).reshape(2, 2, UNIT), ((0, 6), (0, 0), (0, 64 - UNIT))
+    ).reshape(8, 128)
+    wq = w_qkv.reshape(UNIT, 3, 2, 2, 2, 2, 72).transpose(5, 3, 0, 1, 2, 4, 6).reshape(4, UNIT, 864)
+    wq = jnp.pad(wq, ((0, 0), (0, PAD - UNIT), (0, 0)))
+    wg = w_gu.reshape(UNIT, 2, 2, 2, 2, 2, 192).transpose(5, 3, 0, 1, 2, 4, 6).reshape(4, UNIT, 1536)
+    wg = jnp.pad(wg, ((0, 0), (0, PAD - UNIT), (0, 0)))
+    wp = jnp.pad(w_proj, ((0, PAD - UNIT), (0, 0)))
+
+    full = (GROUP, D)
+    (
+        wq_all, wp_all, wg_all, wd_all, ha, rawq, rawk, qr, kr, vv, att, hm, dmlp, tokp, og, attn_out,
+    ) = call(
+        kernel_a, 0,
+        [
+            ((2, 2, 2, 144, 864), BF), ((2, 2, 2, 64, D), BF), ((2, 2, 2, 144, 1536), BF), ((2, 2, 2, 96, D), BF),
+            (full, BF), ((8, 512, 128), F32), ((8, 512, 128), F32), ((8, 512, 128), BF), ((8, 512, 128), BF),
+            ((8, 512, 128), BF), ((GROUP, 512), BF), (full, BF), (full, BF),
+            ((TOK, D), BF), ((TOK, D), BF), ((TOK, D), F32),
+        ],
+        [
+            pltpu.VMEM((4, PAD, 864), BF), pltpu.VMEM((4, PAD, 1536), BF), pltpu.VMEM((TOK, D), BF),
+            pltpu.VMEM((TOK, D), BF), pltpu.VMEM((D, 1536), BF), pltpu.VMEM((3, TOK, D), BF),
+            pltpu.VMEM((3, TOK, D), BF), pltpu.VMEM((TOK, D), F32),
+        ],
+        (
+            tokens.reshape(4, 64, D), cotangent.reshape(4, 64, D), wq, wg, wp, w_down, perm, spread, pick, tabs,
+            gains, modv, bq, bp, maskb, valid,
+        ),
+        hbm=(0, 1, 2, 3),
+    )
+    dwg, dwd, dattn, dmid, bout, small_b, dbg = call(
+        kernel_b, 1,
+        [
+            ((2, 2, 2, 144, 1536), BF), ((2, 2, 2, 96, D), BF), (full, BF), ((TOK, D), F32), ((4, 64, D), BF),
+            ((8, D), F32), ((8, 1536), F32),
+        ],
+        [
+            pltpu.VMEM((TOK, 1536), F32), pltpu.VMEM((GROUP, 1536), BF), pltpu.VMEM((GROUP, 768), BF),
+            pltpu.VMEM((3, TOK, D), BF), pltpu.VMEM((3, TOK, D), BF), pltpu.VMEM((TOK, D), F32),
+            pltpu.VMEM((3, TOK, D), BF), pltpu.VMEM((3, TOK, D), BF), pltpu.VMEM((TOK, D), F32),
+            pltpu.VMEM((TOK, D), BF),
+        ],
+        (wg_all, wd_all, hm, dmlp, tokp, og, attn_out, modv, bg, bd, perm, valid),
+    )
+    dtok, fq, fg, fp, fd, small_c, dbq, dgain = call(
+        kernel_c, 2,
+        [
+            ((4, 64, D), BF), ((4, PAD, 864), BF), ((4, PAD, 1536), BF), ((PAD, D), F32), ((96, D), F32),
+            ((8, D), F32), ((8, 1536), F32), ((8, 128), F32),
+        ],
+        [
+            pltpu.VMEM((2, 2, 2, 144, 864), BF), pltpu.VMEM((2, 2, 2, PAD, D), BF), pltpu.VMEM((GROUP, 512), BF),
+            pltpu.VMEM((GROUP, 1536), BF), pltpu.VMEM((GROUP, 864), BF), pltpu.VMEM((3, TOK, D), BF),
+            pltpu.VMEM((3, TOK, D), BF), pltpu.VMEM((TOK, D), F32), pltpu.VMEM((TOK, D), BF),
+            pltpu.VMEM((4, PAD, 864), BF), pltpu.VMEM((4, PAD, 1536), BF),
+        ]
+        + Reduce.buffers(144, 1536, SPLIT_G) + Reduce.buffers(96, D, SPLIT_D)
+        + Reduce.buffers(144, 864, SPLIT_Q) + Reduce.buffers(PAD, D, SPLIT_P),
+        (
+            dwg, dwd, dattn, att, wp_all, wq_all, ha, rawq, rawk, qr, kr, vv, maskb, dmid, tokp, modv, gains, tabs,
+            perm, spread, pick,
+        ),
+    )
+
+    g_w_qkv = fq[:, :UNIT].reshape(2, 2, UNIT, 3, 2, 2, 72).transpose(2, 3, 4, 1, 5, 0, 6)
+    g_w_qkv = g_w_qkv.reshape(UNIT, 3456).astype(F32)
+    g_w_gu = fg[:, :UNIT].reshape(2, 2, UNIT, 2, 2, 2, 192).transpose(2, 3, 4, 1, 5, 0, 6)
+    g_w_gu = g_w_gu.reshape(UNIT, 6144).astype(F32)
+    spread_own = lambda v: lax.dynamic_update_index_in_dim(
+        jnp.zeros(v.shape[:2] + (2,) + v.shape[2:3] + (2,) + v.shape[3:], F32),
+        lax.dynamic_update_index_in_dim(
+            jnp.zeros(v.shape[:3] + (2,) + v.shape[3:], F32), v[:, :, :, None], zl, 3
+        )[:, :, None],
+        c,
+        2,
+    )
+    db_qkv = spread_own(dbq[0].reshape(3, 2, 2, 2, 64)[..., :UNIT]).reshape(3456)
+    db_gu = spread_own(dbg[0].reshape(2, 2, 2, 2, 96)).reshape(32, 192)
+    vecs = from_order(jnp.stack([small_c[0], small_c[1], small_b[3], small_b[1], small_b[2], small_b[0],
+                                 small_b[5], small_b[4]]))
+    d_mod = vecs[:6].reshape(32, 1, 216)
+    d_mod = lax.dynamic_update_slice(jnp.zeros((32, 16, 216), F32), d_mod, (0, item, 0)).reshape(32, 3456)
+    dg = dgain[:2].reshape(2, 2, 64)[..., :UNIT].reshape(144)
+    pack = jnp.concatenate(
+        [
+            d_mod,
+            db_qkv[: 2 * D].reshape(32, 72),
+            db_qkv[2 * D :].reshape(32, 36),
+            db_gu,
+            vecs[6].reshape(32, UNIT),
+            vecs[7].reshape(32, UNIT),
+            jnp.broadcast_to(dg, (32, 144)),
+        ],
+        1,
+    )
+    pack = lax.psum_scatter(pack, every, scatter_dimension=0, tiled=True)[0]
+    d_mod = pack[:3456].reshape(16, 216)
+    g_b_mod = jnp.sum(d_mod, 0)
+    g_w_mod = jnp.einsum("id,ie->de", act.astype(F32), d_mod, precision=PRECISE)
+    d_act = jnp.einsum("ie,de->id", d_mod, w_mod.astype(F32), precision=PRECISE)
+    sig = jax.nn.sigmoid(cond)
+    d_cond = d_act * sig * (1.0 + cond * (1.0 - sig))
+    d_cond = d_cond.reshape(4, 4, 8, 144).transpose(0, 2, 1, 3).reshape(32, 4, 144)
+    d_cond = lax.psum_scatter(d_cond, every, scatter_dimension=0, tiled=True)[0]
+    return (
+        bout.reshape(tokens.shape),
+        dtok.reshape(tokens.shape).astype(F32),
+        d_cond,
+        g_w_mod,
+        g_b_mod,
+        g_w_qkv,
+        pack[3456:3528],
+        pack[3528:3564],
+        pack[3828:3900],
+        pack[3900:3972],
+        fp[:UNIT],
+        pack[3756:3792],
+        g_w_gu,
+        pack[3564:3756],
+        fd,
+        pack[3792:3828],
+    )
+
+
 def solution(mesh):
     in_specs = (
         P("dp", "row", "col", None),

time: 3020 us -> 906 us (0.30); the launches traced: 2960 us -> 900 us
  blocking collectives: 1450 us -> 13.2 us
  Pallas kernels: 0 us -> 458 us
  waiting for transfers between devices: 684 us -> 356 us
  matrix products: 314 us -> 2.15 us
  local copies, waits for them, and re-layouts: 284 us -> 49.5 us
  starting transfers between devices: 122 us -> 0.12 us
  other arithmetic: 88.2 us -> 5.92 us
    unnamed x3 -> x1, blocking collectives: 1450 us -> 13.2 us
    pallas_call x0 -> x3, Pallas kernels: none -> 458 us  [call(): pl.pallas_call(kernel, out_shape=[jax.ShapeDtypeStruct(s, t) for s, t in...]
    all_gather x6 -> x0, waiting for transfers between devices: 347 us -> none  [the longest x1 106 us: local(): lax.all_gather(w_gu, ('dp', 'row', 'col'), axis=0, tiled=True)]
    dot_general x127 -> x3, matrix products: 314 us -> 2.15 us  [the longest x1 1.6 us: local(): g_w_mod = jnp.einsum('id,ie->de', act.astype(F32), d_mod, precision=PRECISE)]
    unnamed x34 -> x6, waiting for transfers between devices: 46.5 us -> 356 us
    reduce_scatter x2 -> x0, waiting for transfers between devices: 291 us -> none  [the longest x1 291 us: local(): lax.psum_scatter(dkv_term, ('row', 'col'), scatter_dimension=1, tiled=True)]
    unnamed x210 -> x40, local copies, waits for them, and re-layouts: 150 us -> 4.45 us
    unnamed x23 -> x3, starting transfers between devices: 122 us -> 0.12 us
  transfers between devices with their start and end apart: 31 -> 3, of which waited for: 10 -> 3; matrix products, arithmetic and copies ran while one was open for 61% -> 3% of each run, Pallas kernels for 0% -> 0%
where the time goes in v1:
time: 906 us; the launch traced here: 900 us
  Pallas kernels  458 us (51%)
  waiting for transfers between devices  356 us (39%)
  local copies, waits for them, and re-layouts  49.5 us (5%)
  between operations  15.4 us (2%)
  blocking collectives  13.2 us (1%)
    pallas_call x3, Pallas kernels, call(): pl.pallas_call(kernel, out_shape=[jax.ShapeDtypeStruct(s, t) for s, t in...  458 us
    unnamed x6, waiting for transfers between devices  356 us
  transfers between devices with their start and end apart: 3, of which 3 were waited for; matrix products, arithmetic and copies ran while one was open for 3% of the time, Pallas kernels for 0%

profile of v1, /device:TPU:0, one launch (start us, length us, event | category | flops | bytes accessed | tf_op | source)
XLA Modules:
  0.0 900.2 jit_solution(8339402558879020802)
XLA Ops:
  9.5 1.2 dynamic-slice.5
  11.8 13.2 %all-reduce.6 = bf16[18464]{0:T(1024)(128)(2,1)S(1)} all-reduce(bf16[18464]{0:T(1024)(128)(2,1)S(1)} %dynamic-update-slice), channel_id=2, replica_groups=mesh['dp'=4,'row'=4,'col'=2] {'dp'}, use_global_device_ids=true, to_apply=%add.6 | all-reduce | flops 18464 | bytes 73856
  26.2 2.7 concatenate.14
  33.4 1.3 fusion.4
  43.3 114.0 %all-reduce.14.cloned.1.call-done = f32[122496]{0:T(1024)} async-done(((f32[122496]{0:T(1024)}), f32[122496]{0:T(1024)}) %all-reduce.14.cloned.1.call-update) | async-done | bytes 490000
  157.4 1.4 reshape.345
  163.8 204.7 %shard_map.342 = (bf16[2,2,2,144,864]{4,3,2,1,0:T(8,128)(2,1)}, bf16[2,2,2,64,1152]{4,3,2,1,0:T(8,128)(2,1)}, bf16[2,2,2,144,1536]{4,3,2,1,0:T(8,128)(2,1)}, bf1...) custom-call(bf16[4,64,1152]{2,1,0:T(8,128)(2,1)} %bitcast.78, ...), custom_call_target="tpu_custom_call" | custom-call | tf_op jit(solution)/shard_map/pallas_call | solution.py:1078
  368.6 100.8 %shard_map.343 = (bf16[2,2,2,144,1536]{4,3,2,1,0:T(8,128)(2,1)}, bf16[2,2,2,96,1152]{4,3,2,1,0:T(8,128)(2,1)}, bf16[1024,1152]{1,0:T(8,128)(2,1)}, f32[256,1152]...) custom-call(bf16[2,2,2,144,1536]{4,3,2,1,0:T(8,128)(2,1)} %get-tuple-element.47.wg, ...), custom_call_target="tpu_custom_call" | custom-call | tf_op jit(solution)/shard_map/pallas_call | solution.py:1078
  469.4 1.0 fusion.9
  471.1 152.1 %shard_map.344 = (bf16[4,64,1152]{2,1,0:T(8,128)(2,1)}, bf16[4,48,864]{2,1,0:T(8,128)(2,1)}, bf16[4,48,1536]{2,1,0:T(8,128)(2,1)}, f32[48,1152]{1,0:T(8,128)}, f...) custom-call(bf16[2,2,2,144,1536]{4,3,2,1,0:T(8,128)(2,1)} %get-tuple-element.55.dwg, ...), custom_call_target="tpu_custom_call" | custom-call | tf_op jit(solution)/shard_map/pallas_call | solution.py:1078
  629.8 1.2 reshape.327
  631.0 1.0 copy.102
  632.0 2.1 reshape.325
  634.4 1.0 reshape.326
  635.9 2.2 reshape.324
  638.1 1.1 convert.10
  639.9 123.2 %all-reduce.16.cloned.1.call-done = f32[32,3972]{1,0:T(8,128)} async-done(((f32[32,3972]{1,0:T(8,128)}), f32[32,3972]{1,0:T(8,128)}) %all-reduce.16.cloned.1.call-update) | async-done | bytes 508432
  763.1 0.9 dynamic-slice_reduce_fusion
  764.5 1.6 fusion.10
  766.9 1.4 dynamic-slice_bitcast_fusion.4
  768.3 1.4 dynamic-slice_bitcast_fusion.2
  770.2 1.3 dynamic-slice.18
  771.6 119.0 %all-reduce.18.cloned.1.call-done = f32[32,4,144]{2,1,0:T(4,128)} async-done(((f32[32,4,144]{2,1,0:T(4,128)}), f32[32,4,144]{2,1,0:T(4,128)}) %all-reduce.18.cloned.1.call-update) | async-done | bytes 73744
  890.6 1.3 dynamic-slice_bitcast_fusion.1
  (149 shorter events, 33.6 us)
Async XLA Ops:
  7.2 18.6 %copy-start = (bf16[1152,216]{0,1:T(8,128)(2,1)S(1)}, bf16[1152,216]{0,1:T(8,128)(2,1)}, u32[]{:S(2)}) copy-start(bf16[1152,216]{0,1:T(8,128)(2,1)} %param.28) | copy-start | bytes 1492996
  7.2 25.9 %copy-start.12 = (s32[512]{0:T(512)S(1)}, s32[512]{0:T(512)}, u32[]{:S(2)}) copy-start(s32[512]{0:T(512)} %constant.191.clone) | copy-start | bytes 6148
  7.2 26.0 %copy-start.13 = (s32[512]{0:T(512)S(1)}, s32[512]{0:T(512)}, u32[]{:S(2)}) copy-start(s32[512]{0:T(512)} %constant.192.clone) | copy-start | bytes 6148
  7.2 26.0 %copy-start.14 = (f32[72]{0:T(128)S(1)}, f32[72]{0:T(128)}, u32[]{:S(2)}) copy-start(f32[72]{0:T(128)} %param.32) | copy-start | bytes 868
  7.2 26.1 %copy-start.15 = (f32[72]{0:T(128)S(1)}, f32[72]{0:T(128)}, u32[]{:S(2)}) copy-start(f32[72]{0:T(128)} %param.33) | copy-start | bytes 868
  7.2 29.0 %copy-start.4 = (bf16[36,6144]{1,0:T(8,128)(2,1)S(1)}, bf16[36,6144]{1,0:T(8,128)(2,1)}, u32[]{:S(2)}) copy-start(bf16[36,6144]{1,0:T(8,128)(2,1)} %param.36) | copy-start | bytes 1327108
  7.3 150.1 %all-reduce.14.cloned.1.call-start = ((), (), s32[]{:S(2)}) async-start(), calls=%async_computation | async-start | bytes 983040
  29.4 0.8 copy-start.1
  30.2 732.8 %all-reduce.16.cloned.1.call-start = ((), (), s32[]{:S(2)}) async-start(), calls=%async_computation.1 | async-start | bytes 1048576
  37.0 2.1 copy-start.7
  38.2 3.1 copy-start.11
  624.3 4.7 copy-start.6
  629.0 261.6 %all-reduce.18.cloned.1.call-start = ((), (), s32[]{:S(2)}) async-start(), calls=%async_computation.2 | async-start | bytes 262144
  631.0 3.1 copy-start.8
  634.3 3.7 copy-start.2
  635.9 3.3 copy-start.9
  635.9 128.6 %copy-start.10 = (bf16[16,1152]{1,0:T(8,128)(2,1)S(1)}, bf16[16,1152]{1,0:T(8,128)(2,1)}, u32[]{:S(2)}) copy-start(bf16[16,1152]{1,0:T(8,128)(2,1)} %convert_element_type.115) | copy-start | bytes 110596
  638.1 253.8 %copy-start.3 = (bf16[4,64,1152]{2,1,0:T(8,128)(2,1)S(1)}, bf16[4,64,1152]{2,1,0:T(8,128)(2,1)}, u32[]{:S(2)}) copy-start(bf16[4,64,1152]{2,1,0:T(8,128)(2,1)} %get-tuple-element.54) | copy-start | bytes 1769476
  639.2 253.5 %copy-start.5 = (f32[96,1152]{1,0:T(8,128)S(1)}, f32[96,1152]{1,0:T(8,128)}, u32[]{:S(2)}) copy-start(f32[96,1152]{1,0:T(8,128)} %get-tuple-element.124) | copy-start | bytes 1327108
Sparse Core Ops, SparseCore 0:
  30.3 126.9 all-reduce.13
  629.2 133.8 all-reduce.15
  769.2 121.3 all-reduce.17

commit v2 on v1

--- a/solution.py
+++ b/solution.py
@@ -1072,6 +1072,133 @@
     sent()
 
 
+def near(here, r):
+    x = 1 - here.x if r // 4 else here.x
+    c = 1 - here.c if r // 2 % 2 else here.c
+    y = 1 - here.y if r % 2 else here.y
+    return x, c, y, (x * 2 + c, here.z, y)
+
+
+def along_z(here, r):
+    z = (here.z + r) % 4
+    return z, (here.dp, z, here.y)
+
+
+def greet_small(here):
+    bar = pltpu.get_barrier_semaphore()
+    for d in [near(here, r)[3] for r in range(1, 8)] + [along_z(here, r)[1] for r in (1, 2, 3)]:
+        pl.semaphore_signal(bar, inc=1, device_id=d, device_id_type=MESH)
+    pl.semaphore_wait(bar, 10)
+
+
+def kernel_front(cond, w_mod, b_mod, bias, got, condg, msg, p1, m2, ssem, rsem):
+    here = Place()
+    greet_small(here)
+    link = Link(here, ssem, rsem)
+    condg[here.dp] = cond[...]
+    cs = [link.send(cond, condg.at[here.dp], near(here, r)[3]) for r in (2, 4, 6)]
+    for r in range(4):
+        msg[r, 4:6, :] = bias[...]
+    for c in cs:
+        c.wait_recv()
+    v = condg[...].reshape(32, D)
+    act = (v * jax.nn.sigmoid(v)).astype(BF)
+    part = nn(act, w_mod[...]) + b_mod[...]
+    for z in range(4):
+        for d in range(4):
+            msg[z, d : d + 1, 0:216] = part[d * 8 + z : d * 8 + z + 1, :]
+    zs = []
+    for r in (1, 2, 3):
+        z, dev = along_z(here, r)
+        zs.append(link.send(msg.at[z], p1.at[here.z], dev))
+    p1[here.z] = msg[here.z]
+    for c in zs:
+        c.wait_recv()
+    for z in range(4):
+        for d in range(4):
+            m2[d, z, 0:1, :] = p1[z, d : d + 1, :]
+            m2[d, z, 1:3, :] = p1[z, 4:6, :]
+    ns = []
+    for r in range(1, 8):
+        x, _, y, dev = near(here, r)
+        ns.append(link.send(m2.at[x * 2 + y], got.at[here.x, here.c, here.y], dev))
+    got[here.x, here.c, here.y] = m2[here.x * 2 + here.y]
+    for c in ns:
+        c.wait_recv()
+    link.finish()
+
+
+def three(v):
+    hi = v.astype(BF)
+    rest = v - hi.astype(F32)
+    mid = rest.astype(BF)
+    return jnp.concatenate([hi, mid, (rest - mid.astype(F32)).astype(BF)], 0)
+
+
+def kernel_back(pk, condg, w_mod, slope, dwm, sums, dbm, dcond, q1, m2, q2, dm, e0, e1, e2, e3, ssem, rsem):
+    here = Place()
+    greet_small(here)
+    link = Link(here, ssem, rsem)
+    ns = []
+    for r in range(1, 8):
+        x, c, y, dev = near(here, r)
+        ns.append(link.send(pk.at[x, c, y], q1.at[here.x, here.c, here.y], dev))
+    q1[here.x, here.c, here.y] = pk[here.x, here.c, here.y]
+    for n in ns:
+        n.wait_recv()
+    for z in range(4):
+        for x in range(2):
+            for y in range(2):
+                d = x * 2 + y
+                m2[z, d : d + 1, :] = q1[x, 0, y, z, 0:1, :] + q1[x, 1, y, z, 0:1, :]
+        total = q1[0, 0, 0, z, 1:4, :]
+        for i in range(1, 8):
+            total += q1[i // 4, i // 2 % 2, i % 2, z, 1:4, :]
+        m2[z, 4:7, :] = total
+    zs = []
+    for r in (1, 2, 3):
+        z, dev = along_z(here, r)
+        zs.append(link.send(m2.at[z], q2.at[here.z], dev))
+    q2[here.z] = m2[here.z]
+    dm[...] = jnp.zeros_like(dm)
+    v = condg[...].reshape(32, D)
+    act = (v * jax.nn.sigmoid(v)).astype(BF)
+    for c in zs:
+        c.wait_recv()
+    for z in range(4):
+        for d in range(4):
+            dm[d * 8 + z : d * 8 + z + 1, :] = q2[z, d : d + 1, 0:216]
+    sums[...] = q2[0] + q2[1] + q2[2] + q2[3]
+    dbm[...] = jnp.broadcast_to(jnp.sum(dm[...], 0, keepdims=True), (8, 216))
+    d3 = three(dm[...])
+    for b in range(8):
+        t = nt(d3, w_mod[b * 144 : b * 144 + 144, :])
+        t = t[0:32] + t[32:64] + t[64:96]
+        for d in range(4):
+            e0[d, b % 2, b // 2] = t[d * 8 : d * 8 + 8, :]
+    ns = []
+    for r in range(1, 8):
+        x, c, y, dev = near(here, r)
+        ns.append(link.send(e0.at[x * 2 + c, y], e1.at[here.x, here.c, here.y], dev))
+    e1[here.x, here.c, here.y] = e0[here.dp, here.y]
+    dwm[...] = tn(jnp.concatenate([act, act, act], 0), d3)
+    for n in ns:
+        n.wait_recv()
+    total = e1[0, 0, 0]
+    for i in range(1, 8):
+        total += e1[i // 4, i // 2 % 2, i % 2]
+    e2[...] = total
+    zs = []
+    for r in (1, 2, 3):
+        z, dev = along_z(here, r)
+        zs.append(link.send(e2.at[z], e3.at[here.z], dev))
+    e3[here.z] = e2[here.z]
+    for c in zs:
+        c.wait_recv()
+    dcond[...] = (e3[0] + e3[1] + e3[2] + e3[3]) * slope[...]
+    link.finish()
+
+
 def call(kernel, ident, outs, scratch, args, hbm=(), sems=64):
     vm = pl.BlockSpec(memory_space=pltpu.VMEM)
     hb = pl.BlockSpec(memory_space=pltpu.HBM)
@@ -1117,32 +1244,41 @@
     perm, spread, pick, tabs, row_of, col_of = constants()
     dp, z, y = (lax.axis_index(a) for a in every)
     x, c, zh, zl = dp // 2, dp % 2, z // 2, z % 2
-    pack = jnp.concatenate(
-        [conditioning.reshape(-1), heights.astype(BF), widths.astype(BF)]
-    )
-    pack = lax.all_gather(pack, "dp", axis=0)
-    cond = pack[:, : 4 * D].reshape(16, D).astype(F32)
-    tall = pack[:, 4 * D : 4 * D + 4].reshape(16).astype(jnp.int32)
-    wide = pack[:, 4 * D + 4 :].reshape(16).astype(jnp.int32)
-    act = (cond * jax.nn.sigmoid(cond)).astype(BF)
-    part = jnp.dot(act, w_mod, preferred_element_type=F32) + b_mod.astype(F32)
-    pack = jnp.concatenate([part.reshape(-1)] + [b.astype(F32) for b in (b_qkv, b_proj, b_gu, b_down)])
-    pack = lax.all_gather(pack, every, axis=0)
+    block = jnp.concatenate(
+        [
+            conditioning.astype(F32),
+            jnp.pad(jnp.stack([heights, widths]).astype(F32), ((0, 0), (0, D - 4))),
+            jnp.zeros((2, D), F32),
+        ]
+    )
+    bias = jnp.concatenate([b_qkv, b_proj, b_gu, b_down]).astype(F32)
+    bias = jnp.pad(bias, (0, 140)).reshape(2, 256)
+    got, condg = call(
+        kernel_front, 3,
+        [((2, 2, 2, 4, 8, 256), F32), ((4, 8, D), F32)],
+        [pltpu.VMEM((4, 8, 256), F32), pltpu.VMEM((4, 8, 256), F32), pltpu.VMEM((4, 4, 8, 256), F32)],
+        (block, w_mod, b_mod.astype(F32).reshape(1, 216), bias),
+        sems=16,
+    )
+    tall = condg[:, 4, :4].reshape(16)
+    wide = condg[:, 5, :4].reshape(16)
     item = (2 * x + y) * 4 + z
-    modv = lax.dynamic_index_in_dim(pack[:, :3456].reshape(32, 16, 216), item, 1, False)
+    got = got.transpose(0, 1, 3, 2, 4, 5).reshape(32, 8, 256)
+    modv = got[:, 0, :216]
+    pack = got[:, 1:3].reshape(32, 512)
     modv = to_order(modv.reshape(6, D))
     modv = jnp.concatenate([modv, jnp.zeros((2, D), F32)])
     own = lambda v: lax.dynamic_index_in_dim(
         lax.dynamic_index_in_dim(v, c, 2, False), zl, 3, False
     )
-    bq = own(pack[:, 3456:3564].reshape(3, 2, 2, 2, 2, 2, UNIT))
+    bq = own(pack[:, 0:108].reshape(3, 2, 2, 2, 2, 2, UNIT))
     bq = jnp.pad(bq, ((0, 0),) * 4 + ((0, 64 - UNIT),)).reshape(1, 1536)
-    bp = to_order(pack[:, 3564:3600].reshape(1, D))
-    bg = own(pack[:, 3600:3792].reshape(2, 2, 2, 2, 2, 2, 96)).reshape(1, 1536)
-    bd = to_order(pack[:, 3792:3828].reshape(1, D))
+    bp = to_order(pack[:, 108:144].reshape(1, D))
+    bg = own(pack[:, 144:336].reshape(2, 2, 2, 2, 2, 2, 96)).reshape(1, 1536)
+    bd = to_order(pack[:, 336:372].reshape(1, D))
     pair = (2 * x + y) * 4 + 2 * zh + jnp.arange(2)
     row_of, col_of = jnp.asarray(row_of), jnp.asarray(col_of)
-    live = (row_of[None] < tall[pair][:, None]) & (col_of[None] < wide[pair][:, None])
+    live = (row_of[None].astype(F32) < tall[pair][:, None]) & (col_of[None].astype(F32) < wide[pair][:, None])
     maskb = jnp.where(live, 0.0, MASKED).astype(F32).reshape(2, 1, 512)
     valid = lax.dynamic_slice(live[zl].astype(F32), (c * TOK,), (TOK,)).reshape(TOK, 1)
     gains = jnp.pad(
@@ -1226,47 +1362,62 @@
     db_gu = spread_own(dbg[0].reshape(2, 2, 2, 2, 96)).reshape(32, 192)
     vecs = from_order(jnp.stack([small_c[0], small_c[1], small_b[3], small_b[1], small_b[2], small_b[0],
                                  small_b[5], small_b[4]]))
-    d_mod = vecs[:6].reshape(32, 1, 216)
-    d_mod = lax.dynamic_update_slice(jnp.zeros((32, 16, 216), F32), d_mod, (0, item, 0)).reshape(32, 3456)
     dg = dgain[:2].reshape(2, 2, 64)[..., :UNIT].reshape(144)
-    pack = jnp.concatenate(
+    biases = jnp.concatenate(
         [
-            d_mod,
             db_qkv[: 2 * D].reshape(32, 72),
             db_qkv[2 * D :].reshape(32, 36),
             db_gu,
             vecs[6].reshape(32, UNIT),
             vecs[7].reshape(32, UNIT),
-            jnp.broadcast_to(dg, (32, 144)),
+            jnp.zeros((32, 140), F32),
         ],
         1,
-    )
-    pack = lax.psum_scatter(pack, every, scatter_dimension=0, tiled=True)[0]
-    d_mod = pack[:3456].reshape(16, 216)
-    g_b_mod = jnp.sum(d_mod, 0)
-    g_w_mod = jnp.einsum("id,ie->de", act.astype(F32), d_mod, precision=PRECISE)
-    d_act = jnp.einsum("ie,de->id", d_mod, w_mod.astype(F32), precision=PRECISE)
-    sig = jax.nn.sigmoid(cond)
-    d_cond = d_act * sig * (1.0 + cond * (1.0 - sig))
-    d_cond = d_cond.reshape(4, 4, 8, 144).transpose(0, 2, 1, 3).reshape(32, 4, 144)
-    d_cond = lax.psum_scatter(d_cond, every, scatter_dimension=0, tiled=True)[0]
+    ).reshape(32, 2, 256)
+    pack = jnp.concatenate(
+        [
+            jnp.pad(vecs[:6].reshape(32, 1, 216), ((0, 0), (0, 0), (0, 40))),
+            biases,
+            jnp.broadcast_to(jnp.pad(dg, (0, 112)), (32, 1, 256)),
+            jnp.zeros((32, 4, 256), F32),
+        ],
+        1,
+    )
+    pack = pack.reshape(2, 2, 4, 2, 8, 256).transpose(0, 1, 3, 2, 4, 5)
+    cond_f = conditioning.astype(F32)
+    sig = jax.nn.sigmoid(cond_f)
+    slope = lax.dynamic_slice(sig * (1.0 + cond_f * (1.0 - sig)), (0, (z * 2 + y) * 144), (4, 144))
+    slope = jnp.concatenate([slope, jnp.zeros((4, 144), F32)])
+    g_w_mod, sums, g_b_mod, d_cond = call(
+        kernel_back, 4,
+        [((D, 216), F32), ((8, 256), F32), ((8, 216), F32), ((8, 144), F32)],
+        [
+            pltpu.VMEM((2, 2, 2, 4, 8, 256), F32), pltpu.VMEM((4, 8, 256), F32), pltpu.VMEM((4, 8, 256), F32),
+            pltpu.VMEM((32, 216), F32), pltpu.VMEM((4, 2, 4, 8, 144), F32), pltpu.VMEM((2, 2, 2, 4, 8, 144), F32),
+            pltpu.VMEM((4, 8, 144), F32), pltpu.VMEM((4, 8, 144), F32),
+        ],
+        (pack, condg, w_mod, slope),
+        sems=24,
+    )
+    biases = sums[4:6].reshape(512)
+    gains_out = sums[6, :144]
     return (
         bout.reshape(tokens.shape),
         dtok.reshape(tokens.shape).astype(F32),
-        d_cond,
+        d_cond[:4],
         g_w_mod,
-        g_b_mod,
+        g_b_mod[0],
         g_w_qkv,
-        pack[3456:3528],
-        pack[3528:3564],
-        pack[3828:3900],
-        pack[3900:3972],
+        biases[:72],
+        biases[72:108],
+        gains_out[:72],
+        gains_out[72:],
         fp[:UNIT],
-        pack[3756:3792],
+        biases[300:336],
         g_w_gu,
-        pack[3564:3756],
+        biases[108:300],
         fd,
-        pack[3792:3828],
+        biases[336:372],
     )
 
 

time: 906 us -> 562 us (0.62)
  waiting for transfers between devices: 356 us -> 0 us
  Pallas kernels: 458 us -> 503 us
  between operations: 15.4 us -> 1.45 us
  blocking collectives: 13.2 us -> 0 us
    unnamed x6 -> x0, waiting for transfers between devices: 356 us -> none
    pallas_call x3 -> x5, Pallas kernels: 458 us -> 503 us  [call(): pl.pallas_call(kernel, out_shape=[jax.ShapeDtypeStruct(s, t) for s, t in...]
    unnamed x1 -> x0, blocking collectives: 13.2 us -> none
  transfers between devices with their start and end apart: 3 -> 0, of which waited for: 3 -> 0; matrix products, arithmetic and copies ran while one was open for 3% -> 0% of each run, Pallas kernels for 0% -> 0%
where the time goes in v2:
time: 562 us; the launch traced here: 557 us
  Pallas kernels  503 us (90%)
  local copies, waits for them, and re-layouts  43.3 us (8%)
  other arithmetic  9.29 us (2%)
    pallas_call x5, Pallas kernels, call(): pl.pallas_call(kernel, out_shape=[jax.ShapeDtypeStruct(s, t) for s, t in...  503 us

profile of v2, /device:TPU:0, one launch (start us, length us, event | category | flops | bytes accessed | tf_op | source)
XLA Modules:
  0.0 557.1 jit_solution(3350787661601760683)
XLA Ops:
  0.7 2.1 copy.69.w_mod
  6.4 1.2 reshape.308
  7.6 18.0 %shard_map.342 = (f32[2,2,2,4,8,256]{5,4,3,2,1,0:T(8,128)}, f32[4,8,1152]{2,1,0:T(8,128)}) custom-call(f32[8,1152]{1,0:T(8,128)} %fusion.cond, bf16[1152,216]{1,0:T(8,128)(2,1)} %copy.69.w_mod, f32[1,216]{1,0:T(1,128)} %bitcast.93, f32[2,256]{1,0:T(2,128)} %reshape.311.bias), custom_call_target="tpu_custom_call" | custom-call | tf_op jit(solution)/shard_map/pallas_call | solution.py:1205
  25.7 0.8 slice_reduce_fusion.4
  29.3 1.3 fusion.10
  32.0 1.0 copy.70
  38.6 0.9 pad.40.wg_in
  42.4 202.1 %shard_map.343 = (bf16[2,2,2,144,864]{4,3,2,1,0:T(8,128)(2,1)}, bf16[2,2,2,64,1152]{4,3,2,1,0:T(8,128)(2,1)}, bf16[2,2,2,144,1536]{4,3,2,1,0:T(8,128)(2,1)}, bf1...) custom-call(bf16[4,64,1152]{2,1,0:T(8,128)(2,1)} %bitcast.70, ...), custom_call_target="tpu_custom_call" | custom-call | tf_op jit(solution)/shard_map/pallas_call | solution.py:1205
  246.1 101.8 %shard_map.344 = (bf16[2,2,2,144,1536]{4,3,2,1,0:T(8,128)(2,1)}, bf16[2,2,2,96,1152]{4,3,2,1,0:T(8,128)(2,1)}, bf16[1024,1152]{1,0:T(8,128)(2,1)}, f32[256,1152]...) custom-call(bf16[2,2,2,144,1536]{4,3,2,1,0:T(8,128)(2,1)} %get-tuple-element.55.wg, ...), custom_call_target="tpu_custom_call" | custom-call | tf_op jit(solution)/shard_map/pallas_call | solution.py:1205
  347.9 159.4 %shard_map.345 = (bf16[4,64,1152]{2,1,0:T(8,128)(2,1)}, bf16[4,48,864]{2,1,0:T(8,128)(2,1)}, bf16[4,48,1536]{2,1,0:T(8,128)(2,1)}, f32[48,1152]{1,0:T(8,128)}, f...) custom-call(bf16[2,2,2,144,1536]{4,3,2,1,0:T(8,128)(2,1)} %get-tuple-element.63.dwg, ...), custom_call_target="tpu_custom_call" | custom-call | tf_op jit(solution)/shard_map/pallas_call | solution.py:1205
  507.3 1.1 slice_convert_fusion
  509.0 1.2 reshape.316
  510.3 1.0 copy.84
  511.3 2.2 reshape.314
  514.6 0.8 slice_reduce_fusion.2
  515.7 0.8 slice_reduce_fusion.1
  519.6 21.8 %shard_map.346 = (f32[1152,216]{1,0:T(8,128)}, f32[8,256]{1,0:T(8,128)}, f32[8,216]{1,0:T(8,128)}, f32[8,144]{1,0:T(8,128)}) custom-call(f32[2,2,2,4,8,256]{5,4,3,2,1,0:T(8,128)} %maximum_bitcast_fusion.pk, f32[4,8,1152]{2,1,0:T(8,128)} %get-tuple-element.54.condg, bf16[1152,216]{1,0:T(8,128)(2,1)} %copy.69.w_mod, f32[8,144]{1,0:T(8,128)} %concatenate.31.slope), custom_call_target="tpu_custom_call" | custom-call | tf_op jit(solution)/shard_map/pallas_call | solution.py:1205
  541.4 2.6 copy.85
  547.0 1.3 slice_bitcast_fusion.2
  548.3 1.3 slice.154
  549.8 1.0 reshape.315
  551.3 2.2 reshape.313
  553.5 1.1 convert.11
  555.3 0.8 copy.104
  (135 shorter events, 27.9 us)
Async XLA Ops:
  0.6 28.5 %copy-start.10 = (f32[512]{0:T(512)S(1)}, f32[512]{0:T(512)}, u32[]{:S(2)}) copy-start(f32[512]{0:T(512)} %constant.225) | copy-start | bytes 6148
  0.7 28.5 %copy-start.11 = (f32[512]{0:T(512)S(1)}, f32[512]{0:T(512)}, u32[]{:S(2)}) copy-start(f32[512]{0:T(512)} %constant.226) | copy-start | bytes 6148
  2.8 32.9 %copy-start.13 = (f32[72]{0:T(128)S(1)}, f32[72]{0:T(128)}, u32[]{:S(2)}) copy-start(f32[72]{0:T(128)} %param.32) | copy-start | bytes 868
  2.8 33.0 %copy-start.14 = (f32[72]{0:T(128)S(1)}, f32[72]{0:T(128)}, u32[]{:S(2)}) copy-start(f32[72]{0:T(128)} %param.33) | copy-start | bytes 868
  2.8 33.8 %copy-start.2 = (bf16[36,6144]{1,0:T(8,128)(2,1)S(1)}, bf16[36,6144]{1,0:T(8,128)(2,1)}, u32[]{:S(2)}) copy-start(bf16[36,6144]{1,0:T(8,128)(2,1)} %param.36) | copy-start | bytes 1327108
  37.4 2.1 copy-start.4
  38.6 3.1 copy-start.7
  510.3 3.9 copy-start.9
  511.2 7.6 %copy-start.8 = (bf16[4,1152]{1,0:T(4,128)(2,1)S(1)}, bf16[4,1152]{1,0:T(4,128)(2,1)}, u32[]{:S(2)}) copy-start(bf16[4,1152]{1,0:T(4,128)(2,1)} %param.24) | copy-start | bytes 27652
  516.9 32.7 %copy-start.5 = (bf16[4,48,864]{2,1,0:T(8,128)(2,1)S(1)}, bf16[4,48,864]{2,1,0:T(8,128)(2,1)}, u32[]{:S(2)}) copy-start(bf16[4,48,864]{2,1,0:T(8,128)(2,1)} %get-tuple-element.85) | copy-start | bytes 995332
  541.4 5.0 copy-start.12
  549.8 3.7 copy-start
  550.8 3.8 copy-start.6
  551.3 4.0 copy-start.1
  551.3 4.8 copy-start.3
